TPU v7x, 256 devices: a whole 4x4x8 slice. The times are simulated.
256 devices in a mesh: scene: 16 (over y, x), tile: 16 (over z, core).
Axes of the slice: x: 4, y: 4, z: 8, core: 2. Of those that a mesh axis runs over, the one named last changes fastest.
Arguments:
- feats: bfloat16 [256, 32, 32, 1024], P('scene', 'tile'), may hold values from -6 to 6
- occupancy: int32 [256, 4, 4, 4], P('scene'), may hold values from 0 to 1, as said below
- assign: int32 [16, 16], P('scene'), may hold values from 0 to 15, each once within a row
- w_first: bfloat16 [864, 64], replicated, may hold values from -0.21875 to 0.21875
- w_second: bfloat16 [1728, 64], replicated, may hold values from -0.15625 to 0.15625
- grad_out: bfloat16 [256, 16, 16, 1024], P(('scene', 'tile')), may hold values from -6 to 6
Outputs:
- decoded: bfloat16 [256, 16, 16, 1024], P(('scene', 'tile'))
- grad_first: float32 [864, 64], replicated
- grad_second: float32 [1728, 64], replicated
Inputs may be any that keep to these rules, and one draw needn't show every extreme that they name: Each row of assign names every tile index once. `occupancy`: in each scene, the bricks that share one first brick index hold at most 2 occupied ones, and in every scene some such row holds exactly 2.
All inputs are finite; a program needn't handle non-finite values.
Results may differ from a plain program's by a relative error of at most 0.006.
Values may be sent and summed in bfloat16 or wider, within the bound.
A program may use at most 128 MiB of HBM per device.

v0:
```python
import math

import jax
import jax.numpy as jnp
from jax import lax
from jax.sharding import PartitionSpec as P

BRICK = 8


def shifted(value, axis, steps):
    count = lax.axis_size(axis)
    first, last = (max(0, -steps), min(count, count - steps))
    return lax.ppermute(value, axis, [(source, source + steps) for source in range(first, last)])


def upsample(grid, factor):
    grid = jnp.repeat(grid, factor, axis=-3)
    grid = jnp.repeat(grid, factor, axis=-2)
    return jnp.repeat(grid, factor, axis=-1)


def convolve(lhs, rhs, strides, padding, spec):
    return lax.conv_general_dilated(
        lhs,
        rhs,
        strides,
        padding,
        dimension_numbers=("NDHWC", spec, "NDHWC"),
        preferred_element_type=jnp.float32,
    )


def kernel_grad(lhs, rhs, dilation):
    return lax.conv_general_dilated(
        lhs,
        rhs,
        (1, 1, 1),
        "VALID",
        rhs_dilation=(dilation, dilation, dilation),
        dimension_numbers=("CDHWN", "IDHWO", "DHWNC"),
        preferred_element_type=jnp.float32,
    )


def silu_slope(value):
    sig_value = jax.nn.sigmoid(value)
    return sig_value * (1.0 + value * (1.0 - sig_value))


def per_device(feats, occupancy, assign, w_first, w_second, grad_out):
    tiles = lax.axis_size("tile")
    my_tile = lax.axis_index("tile")
    local_scenes, planes, wide_y, lane = feats.shape
    c_full = w_first.shape[0] // 27
    c_half = w_first.shape[1]
    depth = lane // c_full
    half_planes = planes // 2
    half_x = planes * tiles // 2
    half_y = wide_y // 2
    half_z = depth // 2
    edge = BRICK // 2
    kern_first = w_first.reshape(3, 3, 3, c_full, c_half)
    kern_second = w_second.reshape(3, 3, 3, c_half, c_half)
    flipped = kern_second[::-1, ::-1, ::-1]
    order_row = assign[0]
    tile_ids = jnp.arange(tiles, dtype=jnp.int32)
    hits = (order_row[:, None] == tile_ids[None, :]).astype(jnp.int32)
    inverse = jnp.sum(hits * tile_ids[:, None], axis=0)
    plane_ids = (my_tile * planes + jnp.arange(planes, dtype=jnp.int32)) // BRICK
    full_rows = jnp.take(occupancy, plane_ids, axis=1)
    full_mask = jnp.repeat(jnp.repeat(full_rows, BRICK, axis=2), BRICK, axis=3).astype(jnp.bfloat16)
    half_ids = (my_tile * half_planes + jnp.arange(half_planes, dtype=jnp.int32)) // edge
    half_rows = jnp.take(occupancy, half_ids, axis=1)
    tile_mask = jnp.repeat(jnp.repeat(half_rows, edge, axis=2), edge, axis=3).astype(jnp.float32)[
        :, :, :, :, None
    ]
    masked = (
        feats.reshape(local_scenes, planes, wide_y, depth, c_full) * full_mask[:, :, :, :, None]
    )
    rim_layer = shifted(masked[:, planes - 1 :], "tile", 1)
    grad_source = jnp.concatenate([rim_layer, masked], axis=1)
    grad_source = jnp.pad(grad_source, ((0, 0), (0, 0), (1, 0), (1, 0), (0, 0)))
    pre = convolve(grad_source, kern_first, (2, 2, 2), "VALID", "DHWIO")
    hidden = (jax.nn.silu(pre) * tile_mask).astype(jnp.bfloat16)
    own_scene = inverse[my_tile]
    own_occ = lax.dynamic_index_in_dim(occupancy, own_scene, 0, keepdims=True)
    scene_mask = upsample(own_occ, edge).astype(jnp.float32)[:, :, :, :, None]
    outgoing = jnp.take(
        hidden.reshape(local_scenes, half_planes, half_y, half_z * c_half), inverse, axis=0
    )
    whole = lax.all_to_all(outgoing, "tile", split_axis=0, concat_axis=1, tiled=True)
    hidden_scene = whole.reshape(1, half_x, half_y, half_z, c_half)
    second = convolve(hidden_scene, kern_second, (1, 1, 1), [(1, 1), (1, 1), (1, 1)], "DHWIO")
    decoded = (jax.nn.silu(second) * scene_mask).astype(jnp.bfloat16)
    upstream = grad_out.reshape(1, half_x, half_y, half_z, c_half).astype(jnp.float32)
    d_second = (upstream * scene_mask * silu_slope(second)).astype(jnp.bfloat16)
    hidden_pad = jnp.pad(hidden_scene, ((0, 0), (1, 1), (1, 1), (1, 1), (0, 0)))
    part_second = kernel_grad(hidden_pad, d_second, 1)
    d_hidden = convolve(d_second, flipped, (1, 1, 1), [(1, 1), (1, 1), (1, 1)], "DHWOI").astype(
        jnp.bfloat16
    )
    returned = lax.all_to_all(
        d_hidden.reshape(1, half_x, half_y, half_z * c_half),
        "tile",
        split_axis=1,
        concat_axis=0,
        tiled=True,
    )
    returned = jnp.take(returned, order_row, axis=0).reshape(
        local_scenes, half_planes, half_y, half_z, c_half
    )
    d_pre = (returned.astype(jnp.float32) * tile_mask * silu_slope(pre)).astype(jnp.bfloat16)
    part_first = kernel_grad(grad_source, d_pre, 2)
    total_first, total_second = lax.psum((part_first, part_second), ("scene", "tile"))
    factor = 1.0 / math.sqrt(lax.axis_size("scene") * tiles * half_x * half_y * half_z)
    grad_first = (total_first * factor).reshape(27 * c_full, c_half)
    grad_second = (total_second * factor).reshape(27 * c_half, c_half)
    return (decoded.reshape(1, half_x, half_y, half_z * c_half), grad_first, grad_second)


def solution(mesh):
    return jax.shard_map(
        per_device,
        mesh=mesh,
        in_specs=(
            P("scene", "tile", None, None),
            P("scene", None, None, None),
            P("scene", None),
            P(),
            P(),
            P(("scene", "tile"), None, None, None),
        ),
        out_specs=(P(("scene", "tile"), None, None, None), P(), P()),
        check_vma=False,
    )
```

profile of v0, /device:TPU:1, one launch (start us, length us, event | category | flops | bytes accessed | tf_op | source)
XLA Modules:
  0.0 475.6 jit_solution(3048680424161687972)
XLA Ops:
  7.2 1.3 gather_fusion
  8.6 0.1 fusion.35
  8.7 0.1 broadcast_bitcast_fusion
  8.7 11.0 %reshape.229 = bf16[16,2,32,32,32]{4,3,2,1,0:T(8,128)(2,1)} reshape(bf16[16,2,32,1024]{3,2,1,0:T(8,128)(2,1)} %param.8) | data formatting | bytes 4194304 | tf_op jit(solution)/shard_map/reshape | solution.py:79
  19.7 8.2 %copy_multiply_fusion = bf16[16,2,32,32,32]{4,0,3,2,1:T(8,128)(2,1)S(1)} fusion(bf16[16,2,32,32,32]{4,3,2,1,0:T(8,128)(2,1)} %reshape.229, bf16[16,2,32,32]{0,3,2,1:T(8,128)(2,1)S(1)} %broadcast_bitcast_fusion), kind=kLoop, calls=%fused_computation.4 | loop fusion | flops 1048576 | bytes 4259840 | tf_op jit(solution)/shard_map/mul | solution.py:79
  28.0 3.1 slice.26
  31.1 1.4 copy-done
  32.4 4.9 %collective-permute-start = (bf16[16,1,32,32,32]{4,0,3,2,1:T(8,128)(2,1)}, bf16[16,1,32,32,32]{4,0,3,2,1:T(8,128)(2,1)}, u32[]{:S(2)}, u32[]{:S(2)}) collective-permute-start(bf16[16,1,32,32,32]{4,0,3,2,1:T(8,128)(2,1)} %slice.26), channel_id=1, source_target_pairs={{0,1},{1,2},{2,3},{3,4},{4,5},{5,6},{6,7},{7,8},{8,9},{9,10},{10,1... | collective-permute-start | bytes 3145736 | tf_op jit(solution)/shard_map/ppermute | solution.py:14
  37.4 0.2 copy.120
  37.6 0.1 select_reduce_fusion
  37.7 45.4 %collective-permute-done = bf16[16,1,32,32,32]{4,0,3,2,1:T(8,128)(2,1)} collective-permute-done((bf16[16,1,32,32,32]{4,0,3,2,1:T(8,128)(2,1)}, bf16[16,1,32,32,32]{4,0,3,2,1:T(8,128)(2,1)}, u32[]{:S(2)}, u32[]{:S(2)}) %collective-permute-start) | collective-permute-done | bytes 1048608 | tf_op jit(solution)/shard_map/ppermute | solution.py:14
  83.2 11.3 %multiply_convert_fusion = (bf16[16,1,16,16,64]{4,0,3,2,1:T(8,128)(2,1)S(1)}, f32[16,1,16,16,64]{4,0,3,2,1:T(8,128)}) fusion(f32[16,16,16]{0,2,1:T(8,128)S(1)} %bitcast.106, bf16[3,3,3,32,64]{4,3,2,1,0:T(8,128)(2,1)S(1)} %bitcast.104, bf16[16,2,32,32,32]{4,0,3,2,1:T(8,128)(2,1)} %copy-done, bf16[16,1,32,32,32]{4,0,3,2,1:T(8,128)(2,1)} %collective-permute-done), kind=kOutput, calls=%fused_computation.34 | convolution fusion | flops 442171392 | bytes 4845568 | tf_op jit(solution)/shard_map/conv_general_dilated | solution.py:24
  94.4 0.3 copy.121
  94.7 0.7 reshape.346
  95.5 0.6 gather_fusion.1
  96.0 0.9 fusion.34
  97.0 10.9 %all-to-all-start = ((bf16[16,1,16,1024]{3,2,1,0:T(8,128)(2,1)}), bf16[16,1,16,1024]{3,2,1,0:T(8,128)(2,1)S(1)}, u32[]{:S(2)}, u32[]{:S(2)}) async-start(bf16[16,1,16,1024]{3,2,1,0:T(8,128)(2,1)} %fusion.34), calls=%async_computation | async-start | bytes 1048576 | tf_op jit(solution)/shard_map/all_to_all | solution.py:92
  107.9 0.6 dynamic_slice.7
  109.8 1.0 copy.147
  111.4 0.1 dynamic-slice_convert_fusion
  111.5 0.2 copy.148
  111.7 0.1 broadcast_in_dim.66
  111.8 0.1 convert_element_type.117
  112.0 0.6 copy-done.4
  112.7 0.1 copy.132
  112.8 0.6 reshape.282
  113.4 0.6 pad_clamp_fusion
  114.0 0.5 compare_and_fusion
  114.5 10.6 %all-to-all-done = bf16[16,1,16,1024]{3,2,1,0:T(8,128)(2,1)S(1)} async-done(((bf16[16,1,16,1024]{3,2,1,0:T(8,128)(2,1)}), bf16[16,1,16,1024]{3,2,1,0:T(8,128)(2,1)S(1)}, u32[]{:S(2)}, u32[]{:S(2)}) %all-to-all-start) | async-done | bytes 524320 | tf_op jit(solution)/shard_map/all_to_all | solution.py:92
  125.1 1.7 reshape.285
  126.8 1.5 copy.150
  128.3 0.3 pad.6.clone
  128.7 0.4 copy.125
  129.1 0.3 slice.27
  129.4 0.3 copy-done.8
  129.7 7.7 %add_multiply_fusion = (f32[16,16,8,3,64]{4,2,3,1,0:T(8,128)S(1)}, f32[16,16,8,3,64]{4,2,3,1,0:T(8,128)}) fusion(pred[8,3]{0,1:T(4,128)(4,1)S(1)} %copy-done.16, bf16[3,3,3,64,64]{4,3,2,1,0:T(8,128)(2,1)S(1)} %bitcast.101, bf16[16,16,1,7,2,64]{5,3,4,1,0,2:T(8,128)(2,1)S(1)} %slice.27, bf16[16,16,1,8,3,64]{5,3,4,1,0,2:T(8,128)(2,1)S(1)} %copy.125), kind=kOutput, calls=%fused_computation.11 | convolution fusion | flops 1255538688 | bytes 4612120 | tf_op jit(solution)/shard_map/conv_general_dilated | solution.py:24
  137.4 0.5 copy.133
  137.9 0.1 slice.29
  138.1 1.7 fusion.21
  139.8 1.0 copy-done.1
  140.7 0.3 copy.151
  141.0 0.3 pad.8.clone
  141.3 0.4 copy.137
  141.8 0.3 slice.30
  142.1 11.3 %select_convert_fusion = bf16[16,16,8,3,64]{4,2,3,1,0:T(8,128)(2,1)S(1)} fusion(pred[8,3]{0,1:T(4,128)(4,1)S(1)} %copy-done.16, bf16[3,3,3,64,64]{4,3,2,1,0:T(8,128)(2,1)S(1)} %bitcast.102, bf16[16,16,1,7,2,64]{5,3,4,1,0,2:T(8,128)(2,1)S(1)} %slice.30, bf16[16,16,1,8,3,64]{5,3,4,1,0,2:T(8,128)(2,1)S(1)} %copy.137), kind=kOutput, calls=%fused_computation.10 | convolution fusion | flops 1252786176 | bytes 2252824 | tf_op jit(solution)/shard_map/conv_general_dilated | solution.py:24
  153.4 0.4 copy.139
  153.8 0.2 slice.31
  154.0 0.3 copy.140
  154.3 1.5 reshape.235
  155.8 4.1 all-to-all-start.1
  160.0 3.7 reshape.355
  163.7 26.7 %fusion.24 = f32[3,3,3,64,64]{4,3,2,1,0:T(8,128)} fusion(bf16[1,16,16,16,64]{4,0,3,2,1:T(2,128)(2,1)} %reshape.355, bf16[1,16,16,16,64]{4,3,2,1,0:T(8,128)(2,1)S(1)} %copy-done.2), kind=kOutput, calls=%fused_computation.36 | convolution fusion | flops 797376512 | bytes 1490944 | tf_op jit(solution)/shard_map/conv_general_dilated | solution.py:35
  190.5 1.7 gather_fusion.2
  192.2 0.1 fusion.33
  192.4 1.9 reshape.283
  194.2 13.6 %fusion = f32[3,3,3,32,64]{4,3,2,1,0:T(8,128)} fusion(bf16[16,2,32,32,32]{4,0,3,2,1:T(8,128)(2,1)} %copy-done, bf16[16,1,32,32,32]{4,0,3,2,1:T(8,128)(2,1)} %collective-permute-done, f32[16,1,16,16,64]{4,3,2,0,1:T(8,128)} %reshape.283, f32[16,1,16,16,64]{4,0,3,2,1:T(8,128)} %get-tuple-element.38, f32[16,16,16]{0,2,1:T(8,128)S(1)} %bitcast.107), kind=kOutput, calls=%fused_computation.5 | convolution fusion | flops 443219968 | bytes 5480448 | tf_op jit(solution)/shard_map/conv_general_dilated | solution.py:35
  207.9 0.5 copy.127
  208.5 0.7 fusion.19
  209.2 0.3 copy.131
  209.5 1.5 reshape.234
  211.0 254.1 %all-reduce.3.cloned.1.call-done = (f32[3,3,3,32,64]{4,3,2,1,0:T(8,128)}, f32[3,3,3,64,64]{4,3,2,1,0:T(8,128)}) async-done(((f32[3,3,3,32,64]{4,3,2,1,0:T(8,128)}, f32[3,3,3,64,64]{4,3,2,1,0:T(8,128)}), (f32[3,3,3,32,64]{4,3,2,1,0:T(8,128)}, f32[3,3,3,64,64]{4,3,2,1,0:T(8,128)})) %all-reduce.3.cloned.1.call-update) | async-done | bytes 663568 | tf_op jit(solution)/shard_map/psum | solution.py:115
  465.1 1.3 broadcast_multiply_fusion
  466.4 1.1 copy.146
  467.5 0.9 copy.145
  (49 shorter events, 0.4 us)
Async XLA Ops:
  27.9 4.5 copy-start
  27.9 9.5 %copy-start.13 = (bf16[864,64]{0,1:T(8,128)(2,1)S(1)}, bf16[864,64]{0,1:T(8,128)(2,1)}, u32[]{:S(2)}) copy-start(bf16[864,64]{0,1:T(8,128)(2,1)} %param.11) | copy-start | bytes 331780
  28.0 9.6 %copy-start.15 = (s32[1,16]{1,0:T(1,128)S(1)}, s32[1,16]{1,0:T(1,128)}, u32[]{:S(2)}) copy-start(s32[1,16]{1,0:T(1,128)} %param.10) | copy-start | bytes 196
  28.0 9.7 %copy-start.9 = (s32[16,4,4,4]{0,3,2,1:T(4,128)S(1)}, s32[16,4,4,4]{0,3,2,1:T(4,128)}, u32[]{:S(2)}) copy-start(s32[16,4,4,4]{0,3,2,1:T(4,128)} %param.9) | copy-start | bytes 12292
  32.4 50.7 %collective-permute-start = (bf16[16,1,32,32,32]{4,0,3,2,1:T(8,128)(2,1)}, bf16[16,1,32,32,32]{4,0,3,2,1:T(8,128)(2,1)}, u32[]{:S(2)}, u32[]{:S(2)}) collective-permute-start(bf16[16,1,32,32,32]{4,0,3,2,1:T(8,128)(2,1)} %slice.26), channel_id=1, source_target_pairs={{0,1},{1,2},{2,3},{3,4},{4,5},{5,6},{6,7},{7,8},{8,9},{9,10},{10,1... | collective-permute-start | bytes 3145736 | tf_op jit(solution)/shard_map/ppermute | solution.py:14
  83.1 11.3 %copy-start.11 = (f32[16,16,4,4]{0,3,2,1:T(4,128)}, f32[16,16,4,4]{0,3,2,1:T(4,128)S(1)}, u32[]{:S(2)}) copy-start(f32[16,16,4,4]{0,3,2,1:T(4,128)S(1)} %broadcast_in_dim.65) | copy-start | bytes 49156
  94.7 15.1 %copy-start.10 = (bf16[1728,64]{0,1:T(8,128)(2,1)S(1)}, bf16[1728,64]{0,1:T(8,128)(2,1)}, u32[]{:S(2)}) copy-start(bf16[1728,64]{0,1:T(8,128)(2,1)} %param.12) | copy-start | bytes 663556
  95.4 17.3 %copy-start.6 = (bf16[1,16,16,1024]{3,2,1,0:T(8,128)(2,1)S(1)}, bf16[1,16,16,1024]{3,2,1,0:T(8,128)(2,1)}, u32[]{:S(2)}) copy-start(bf16[1,16,16,1024]{3,2,1,0:T(8,128)(2,1)} %param.13) | copy-start | bytes 1572868
  97.0 28.2 %all-to-all-start = ((bf16[16,1,16,1024]{3,2,1,0:T(8,128)(2,1)}), bf16[16,1,16,1024]{3,2,1,0:T(8,128)(2,1)S(1)}, u32[]{:S(2)}, u32[]{:S(2)}) async-start(bf16[16,1,16,1024]{3,2,1,0:T(8,128)(2,1)} %fusion.34), calls=%async_computation | async-start | bytes 1048576 | tf_op jit(solution)/shard_map/all_to_all | solution.py:92
  112.0 0.7 copy-start.4
  128.7 1.0 copy-start.8
  128.7 1.0 copy-start.16
  139.7 1.0 copy-start.1
  154.3 9.4 %copy-start.2 = (bf16[1,16,16,16,64]{4,3,2,1,0:T(8,128)(2,1)S(1)}, bf16[1,16,16,16,64]{4,3,2,1,0:T(8,128)(2,1)}, u32[]{:S(2)}) copy-start(bf16[1,16,16,16,64]{4,3,2,1,0:T(8,128)(2,1)} %copy-done.1) | copy-start | bytes 1572868
  155.8 34.6 %all-to-all-start.1 = ((bf16[1,16,16,1024]{3,2,0,1:T(8,128)(2,1)}), bf16[1,16,16,1024]{3,2,0,1:T(8,128)(2,1)}, u32[]{:S(2)}, u32[]{:S(2)}) async-start(bf16[1,16,16,1024]{3,2,0,1:T(8,128)(2,1)} %bitcast.28), calls=%async_computation.1 | async-start | bytes 1048576 | tf_op jit(solution)/shard_map/all_to_all | solution.py:103
  160.0 305.1 %all-reduce.3.cloned.1.call-start = ((), (), s32[]{:S(2)}) async-start(), calls=%async_computation.2 | async-start | bytes 2654208 | tf_op jit(solution)/shard_map/psum | solution.py:115
  163.7 28.5 %copy-start.14 = (pred[16]{0:T(512)(128)(4,1)S(1)}, pred[16]{0:T(512)(128)(4,1)}, u32[]{:S(2)}) copy-start(pred[16]{0:T(512)(128)(4,1)} %compare_and_fusion) | copy-start | bytes 52
  192.2 2.0 copy-start.12
  194.2 13.6 %copy-start.5 = (f32[16,16,4,4]{1,0,3,2:T(8,128)S(1)}, f32[16,16,4,4]{1,0,3,2:T(8,128)}, u32[]{:S(2)}) copy-start(f32[16,16,4,4]{1,0,3,2:T(8,128)} %copy-done.4) | copy-start | bytes 49156
  194.2 13.7 %copy-start.3 = (f32[16,16,8,3,64]{4,2,3,1,0:T(8,128)S(1)}, f32[16,16,8,3,64]{4,2,3,1,0:T(8,128)}, u32[]{:S(2)}) copy-start(f32[16,16,8,3,64]{4,2,3,1,0:T(8,128)} %get-tuple-element.36) | copy-start | bytes 4718596
  465.1 2.3 copy-start.7
Sparse Core Ops, SparseCore 0:
  208.0 257.1 all-reduce.2
where the time goes:
time: 483 us; the launch traced here: 476 us
  waiting for transfers between devices  310 us (64%)
  matrix products  70.6 us (15%)
  local copies, waits for them, and re-layouts  43.5 us (9%)
  starting transfers between devices  20.1 us (4%)
  between operations  16.9 us (3%)
  other arithmetic  14.4 us (3%)
    psum x1, waiting for transfers between devices, per_device(): lax.psum((part_first, part_second), ('scene', 'tile'))  254 us
    ppermute x1, waiting for transfers between devices, shifted(): lax.ppermute(value, axis, [(source, source + steps) for source in range(f...  45.4 us
    conv_general_dilated x2, matrix products, kernel_grad(): lax.conv_general_dilated(lhs, rhs, (1, 1, 1), 'VALID', rhs_dilation=(dila...  40.3 us
    conv_general_dilated x3, matrix products, convolve(): lax.conv_general_dilated(lhs, rhs, strides, padding, dimension_numbers=('...  30.3 us
    reshape x1, local copies, waits for them, and re-layouts, per_device(): feats.reshape(local_scenes, planes, wide_y, depth, c_full)  11 us
    all_to_all x1, starting transfers between devices, per_device(): lax.all_to_all(outgoing, 'tile', split_axis=0, concat_axis=1, tiled=True)  10.9 us
    all_to_all x1, waiting for transfers between devices, per_device(): lax.all_to_all(outgoing, 'tile', split_axis=0, concat_axis=1, tiled=True)  10.6 us
  transfers between devices with their start and end apart: 4, of which 3 were waited for; matrix products, arithmetic and copies ran while one was open for 8% of the time, Pallas kernels for 0%

commit v1 on v0

v1 whole, which is shorter than its diff:
```python
import functools
import math

import jax
import jax.numpy as jnp
from jax import lax
from jax.experimental import pallas as pl
from jax.experimental.pallas import tpu as pltpu
from jax.sharding import PartitionSpec as P

MESH = pl.DeviceIdType.MESH
F32, BF16, I32 = jnp.float32, jnp.bfloat16, jnp.int32
SCENES, BX, SLOTS, NB = 16, 4, 2, 8
NONE = 16
TAPS = [(kx, ky) for kx in range(3) for ky in range(3)]
CHUNK = 48
VMEM_LIMIT = 60 * 1024 * 1024


def vmem():
    return pl.BlockSpec(memory_space=pltpu.VMEM)


def smem():
    return pl.BlockSpec(memory_space=pltpu.SMEM)


def pack_kernel(order_ref, code_ref, feats_ref, out_ref):
    @pl.loop(0, SCENES)
    def _(target):
        scene = order_ref[target]
        rows = []
        for slot in range(SLOTS):
            code = code_ref[target * SLOTS + slot]
            by = code // 4
            bz = code - 4 * by
            for plane in range(2):
                wide = feats_ref[scene, plane, :, pl.ds(pl.multiple_of(bz * 256, 256), 256)].astype(F32)
                acc = jnp.zeros((8, 256), F32)
                for k in range(4):
                    acc = jnp.where(by == k, wide[8 * k : 8 * k + 8], acc)
                rows.append(acc)
        out_ref[target] = jnp.concatenate(rows, axis=0).astype(BF16)


def pack(order, code, feats):
    return pl.pallas_call(
        pack_kernel,
        out_shape=jax.ShapeDtypeStruct((SCENES, 32, 256), BF16),
        in_specs=[smem(), smem(), vmem()],
        out_specs=vmem(),
        compiler_params=pltpu.CompilerParams(vmem_limit_bytes=VMEM_LIMIT),
        name="pack",
    )(order, code, feats)


def relayout_kernel(stage, out_ref, send_sem, recv_sem):
    me = lax.axis_index("tile")
    barrier = pltpu.get_barrier_semaphore()
    for step in range(1, SCENES):
        peer = lax.rem(me + step, SCENES)
        pl.semaphore_signal(barrier, inc=1, device_id={"tile": peer}, device_id_type=MESH)
    out_ref[me] = stage[me]
    pl.semaphore_wait(barrier, SCENES - 1)
    copies = []
    for step in range(1, SCENES):
        peer = lax.rem(me + step, SCENES)
        copy = pltpu.make_async_remote_copy(
            src_ref=stage.at[peer],
            dst_ref=out_ref.at[me],
            send_sem=send_sem.at[step],
            recv_sem=recv_sem.at[step],
            device_id={"tile": peer},
            device_id_type=MESH,
        )
        copy.start()
        copies.append(copy)
    for copy in copies:
        copy.wait_recv()
    for copy in copies:
        copy.wait_send()


def relayout(stage):
    return pl.pallas_call(
        relayout_kernel,
        out_shape=jax.ShapeDtypeStruct((SCENES, 32, 256), BF16),
        in_specs=[vmem()],
        out_specs=vmem(),
        scratch_shapes=[
            pltpu.SemaphoreType.DMA((SCENES,)),
            pltpu.SemaphoreType.DMA((SCENES,)),
        ],
        compiler_params=pltpu.CompilerParams(collective_id=0, has_side_effects=True, vmem_limit_bytes=VMEM_LIMIT),
        name="relayout",
    )(stage)


def iota(shape, dim):
    return lax.broadcasted_iota(I32, shape, dim)


def dot(lhs, rhs, dims=((1,), (0,))):
    return lax.dot_general(lhs, rhs, (dims, ((), ())), preferred_element_type=F32)


def sublane_gather(value, picker):
    index, hit = picker
    pieces = []
    for at in range(0, value.shape[1], 128):
        got = jnp.take_along_axis(value[:, at : at + 128], index, axis=0)
        pieces.append(jnp.where(hit, got, 0.0))
    return pieces[0] if len(pieces) == 1 else jnp.concatenate(pieces, axis=1)


def scene_kernel(code_ref, bricks_ref, w1_ref, w2_ref, w3_ref, cot_ref, dec_ref, pay_ref,
                 fe, he, de, wide1, wide2, wide3, p1, p2, p3):
    codes = [code_ref[b] for b in range(NB)]
    valid = [code < NONE for code in codes]
    bys = [code // 4 for code in codes]
    bzs = [code - 4 * by for code, by in zip(codes, bys)]
    place = [
        jnp.where(valid[b], (b // 2) * 64 + bys[b] * 8 + bzs[b], -10000 * (b + 1)) for b in range(NB)
    ]
    sub = iota((8, 128), 0)
    own = jnp.zeros((8, 128), I32)
    for b in range(NB):
        own = jnp.where(sub == b, place[b], own)

    def picker(dx, dy, dz):
        target = own + (dx * 64 + dy * 8 + dz)
        index = jnp.zeros((8, 128), I32)
        hit = sub < 0
        for b in range(NB):
            same = target == place[b]
            index = jnp.where(same, b, index)
            hit = hit | same
        return index, hit

    pick = {
        (dx, dy, dz): picker(dx, dy, dz)
        for dx in (-1, 0, 1) for dy in (-1, 0, 1) for dz in (-1, 0, 1) if (dx, dy, dz) != (0, 0, 0)
    }

    wide1[...] = jnp.zeros_like(wide1)
    wide2[...] = jnp.zeros_like(wide2)
    wide3[...] = jnp.zeros_like(wide3)
    for tap in range(9):
        base = tap * 384
        w = w1_ref[tap * 96 : tap * 96 + 96, :]
        wide1[base + 352 : base + 384, 0:64] = w[0:32]
        wide1[base : base + 64, 0:64] = w[32:96]
        for zo in range(1, 4):
            at = base + 32 * (2 * zo - 1)
            wide1[at : at + 96, 64 * zo : 64 * zo + 64] = w
        for source, target in ((w2_ref, wide2), (w3_ref, wide3)):
            w = source[tap * 192 : tap * 192 + 192, :]
            target[base + 320 : base + 384, 0:64] = w[0:64]
            target[base : base + 128, 0:64] = w[64:192]
            target[base : base + 192, 64:128] = w
            target[base + 64 : base + 256, 128:192] = w
            target[base + 128 : base + 256, 192:256] = w[0:128]
            target[base + 256 : base + 320, 192:256] = w[128:192]

    row, col = iota((128, 128), 0), iota((128, 128), 1)
    source = ((row // 2) % 4) * 32 + (row % 2) * 16 + (row // 64) * 8 + (row // 8) % 8
    perm = jnp.where(col == source, 1.0, 0.0).astype(BF16)
    for j in range(4):
        stack = jnp.concatenate([bricks_ref[4 * bx + j] for bx in range(BX)], axis=0)
        moved = dot(perm, stack).reshape(2, 8, 8, 256)
        for plane in range(2):
            fe[2 * j + plane + 1, 1:9, :, 0:256] = moved[plane]
    for px in range(-1, 8):
        for py in range(-1, 8):
            dx, dy = (-1 if px < 0 else 0), (-1 if py < 0 else 0)
            tile = fe[px % 8 + 1, py % 8 + 1, :, 0:256]
            if dx or dy:
                fe[px + 1, py + 1, :, 0:256] = sublane_gather(tile, pick[dx, dy, 0])
            fe[px + 1, py + 1, :, 256:384] = sublane_gather(tile[:, 128:256], pick[dx, dy, -1])
    for tap, (kx, ky) in enumerate(TAPS):
        rows = [fe[2 * x + kx, 2 * y + ky] for x in range(4) for y in range(4)]
        p1[:, tap * 384 : tap * 384 + 384] = jnp.concatenate(rows, axis=0).astype(BF16)
    pre = dot(p1[...], wide1[...])

    low = iota((8, 128), 1) < 64

    def extend(value, ext, patches):
        for x in range(4):
            for y in range(4):
                at = (x * 4 + y) * 8
                ext[x + 1, y + 1, :, 0:256] = value[at : at + 8]
        for px in range(-1, 5):
            for py in range(-1, 5):
                dx = -1 if px < 0 else (1 if px > 3 else 0)
                dy = -1 if py < 0 else (1 if py > 3 else 0)
                at = ((px % 4) * 4 + py % 4) * 8
                tile = value[at : at + 8]
                if dx or dy:
                    ext[px + 1, py + 1, :, 0:256] = sublane_gather(tile, pick[dx, dy, 0])
                above = sublane_gather(tile[:, 0:128], pick[dx, dy, 1])
                below = sublane_gather(tile[:, 128:256], pick[dx, dy, -1])
                ext[px + 1, py + 1, :, 256:384] = jnp.where(low, above, below)
        for tap, (kx, ky) in enumerate(TAPS):
            rows = [ext[x + kx, y + ky] for x in range(4) for y in range(4)]
            patches[:, tap * 384 : tap * 384 + 384] = jnp.concatenate(rows, axis=0).astype(BF16)

    sig_pre = jax.nn.sigmoid(pre)
    hidden = (pre * sig_pre).astype(BF16)
    extend(hidden.astype(F32), he, p2)
    second = dot(p2[...], wide2[...])
    sig = jax.nn.sigmoid(second)
    decoded = (second * sig).astype(BF16)

    row, col = iota((32, 128), 0), iota((32, 128), 1)
    goal = jnp.full((32, 128), -1, I32)
    row_t, col_t = iota((128, 32), 0), iota((128, 32), 1)
    goal_t = jnp.full((128, 32), -1, I32)
    for b in range(NB):
        start = jnp.where(valid[b], 16 * b + 4 * bys[b], -10000)
        goal = jnp.where(row % 8 == b, start + row // 8, goal)
        goal_t = jnp.where(col_t % 8 == b, start + col_t // 8, goal_t)
    take = jnp.where(col == goal, 1.0, 0.0).astype(BF16)
    give = jnp.where(row_t == goal_t, 1.0, 0.0).astype(BF16)
    ups = []
    for x in range(4):
        planes = []
        for b in range(NB):
            lane = pl.multiple_of(jnp.where(valid[b], bzs[b], 0) * 256, 256)
            planes.append(cot_ref[4 * (b // 2) + x, :, pl.ds(lane, 256)])
        ups.append(dot(take, jnp.concatenate(planes, axis=0)))
        spread = dot(give, decoded[32 * x : 32 * x + 32])
        for bx in range(BX):
            first, other = spread[32 * bx : 32 * bx + 16], spread[32 * bx + 16 : 32 * bx + 32]
            for c in range(4):
                block = jnp.where(bzs[2 * bx] == c, first, 0.0) + jnp.where(bzs[2 * bx + 1] == c, other, 0.0)
                dec_ref[4 * bx + x, :, 256 * c : 256 * c + 256] = block.astype(BF16)
    upstream = jnp.concatenate(ups, axis=0)

    d_second = (upstream * (sig * (1.0 + second * (1.0 - sig)))).astype(BF16)
    extend(d_second.astype(F32), de, p3)
    d_hidden = dot(p3[...], wide3[...]).astype(BF16)
    d_pre = (d_hidden.astype(F32) * (sig_pre * (1.0 + pre * (1.0 - sig_pre)))).astype(BF16)

    def fold(parts, target):
        half = parts[0].shape[0] // 2
        lo, hi = parts[0] + parts[2], parts[1] + parts[3]
        is_low = iota((half, 128), 1) < 64
        keep = jnp.where(is_low, lo[:half], hi[half:])
        turn = jnp.where(is_low, lo[half:], hi[:half])
        pay_ref[target : target + half, :] = keep + pltpu.roll(turn, 64, 1)

    for tap in range(9):
        full = dot(p1[:, tap * 384 : tap * 384 + 384], d_pre, ((0,), (0,)))
        parts = [jnp.concatenate([full[352:384, 0:128], full[0:64, 0:128]], axis=0)]
        for zo in range(1, 4):
            at, lane = 32 * (2 * zo - 1), 128 * (zo // 2)
            parts.append(full[at : at + 96, lane : lane + 128])
        fold(parts, tap * 48)
        full = dot(p2[:, tap * 384 : tap * 384 + 384], d_second, ((0,), (0,)))
        parts = [
            jnp.concatenate([full[320:384, 0:128], full[0:128, 0:128]], axis=0),
            full[0:192, 0:128],
            full[64:256, 128:256],
            full[128:320, 128:256],
        ]
        fold(parts, 432 + tap * 96)
    pay_ref[1296:1536, :] = jnp.zeros((240, 128), F32)


def scene_step(code, bricks, w1, w2, w3, cot):
    wide = pltpu.VMEM((3456, 256), BF16)
    patch = pltpu.VMEM((128, 3456), BF16)
    return pl.pallas_call(
        scene_kernel,
        out_shape=[
            jax.ShapeDtypeStruct((16, 16, 1024), BF16),
            jax.ShapeDtypeStruct((32 * CHUNK, 128), F32),
        ],
        in_specs=[smem()] + [vmem()] * 5,
        out_specs=[vmem(), vmem()],
        scratch_shapes=[
            pltpu.VMEM((9, 9, 8, 384), F32),
            pltpu.VMEM((6, 6, 8, 384), F32),
            pltpu.VMEM((6, 6, 8, 384), F32),
            wide, wide, wide, patch, patch, patch,
        ],
        compiler_params=pltpu.CompilerParams(vmem_limit_bytes=VMEM_LIMIT),
        name="scene_step",
    )(code, bricks, w1, w2, w3, cot)


def total_kernel(factor, pay_ref, out_ref, from_core, mine, from_scene, part, from_z,
                 core_send, core_recv, scene_send, scene_recv, z_send, z_recv,
                 out_send, out_recv, back_send, back_recv):
    tile, scene = lax.axis_index("tile"), lax.axis_index("scene")
    core = lax.rem(tile, 2)
    z = tile // 2
    sibling = 2 * z + 1 - core

    def to_core():
        return {"tile": sibling}

    def to_scene(peer):
        return {"scene": peer}

    def to_z(peer):
        return {"tile": 2 * peer + core}

    barrier = pltpu.get_barrier_semaphore()
    pl.semaphore_signal(barrier, inc=1, device_id=to_core(), device_id_type=MESH)
    for step in range(1, 16):
        pl.semaphore_signal(barrier, inc=1, device_id=to_scene(lax.rem(scene + step, 16)), device_id_type=MESH)
    for step in range(1, 8):
        pl.semaphore_signal(barrier, inc=1, device_id=to_z(lax.rem(z + step, 8)), device_id_type=MESH)
    pl.semaphore_wait(barrier, 23)

    def remote(src, dst, send, recv, device):
        return pltpu.make_async_remote_copy(
            src_ref=src, dst_ref=dst, send_sem=send, recv_sem=recv, device_id=device, device_id_type=MESH
        )

    waits = []
    cores = []
    for step in range(16):
        owner = lax.rem(scene + step, 16)
        copy = remote(
            pay_ref.at[1 - core, owner], from_core.at[owner], core_send.at[step], core_recv.at[step], to_core()
        )
        copy.start()
        cores.append(copy)
    waits += cores
    scenes = []
    for step in list(range(1, 16)) + [0]:
        owner = lax.rem(scene + step, 16)
        cores[step].wait_recv()
        added = pay_ref[core, owner] + from_core[owner]
        if step == 0:
            from_scene[scene] = added
            continue
        mine[owner] = added
        copy = remote(
            mine.at[owner], from_scene.at[scene], scene_send.at[step], scene_recv.at[step], to_scene(owner)
        )
        copy.start()
        scenes.append(copy)
    waits += scenes
    for copy in scenes:
        copy.wait_recv()
    total = from_scene[0]
    for k in range(1, 16):
        total = total + from_scene[k]
    part[...] = total
    from_z[z] = total
    zs = []
    for step in range(1, 8):
        copy = remote(
            part, from_z.at[z], z_send.at[step], z_recv.at[step], to_z(lax.rem(z + step, 8))
        )
        copy.start()
        zs.append(copy)
    waits += zs
    for copy in zs:
        copy.wait_recv()
    total = from_z[0]
    for k in range(1, 8):
        total = total + from_z[k]
    out_ref[core, scene] = total * factor
    outs = [None]
    backs = []
    for step in range(1, 16):
        copy = remote(
            out_ref.at[core, scene], out_ref.at[core, scene], out_send.at[step], out_recv.at[step],
            to_scene(lax.rem(scene + step, 16)),
        )
        copy.start()
        outs.append(copy)
    for step in range(16):
        owner = lax.rem(scene - step + 16, 16)
        if step:
            outs[step].wait_recv()
        copy = remote(
            out_ref.at[core, owner], out_ref.at[core, owner], back_send.at[step], back_recv.at[step], to_core()
        )
        copy.start()
        backs.append(copy)
    for copy in backs:
        copy.wait_recv()
    for copy in waits + outs[1:] + backs:
        copy.wait_send()


def total_over_devices(payload, factor):
    sem = lambda n: pltpu.SemaphoreType.DMA((n,))
    return pl.pallas_call(
        functools.partial(total_kernel, factor),
        out_shape=jax.ShapeDtypeStruct((2, 16, CHUNK, 128), F32),
        in_specs=[vmem()],
        out_specs=vmem(),
        scratch_shapes=[
            pltpu.VMEM((16, CHUNK, 128), F32),
            pltpu.VMEM((16, CHUNK, 128), F32),
            pltpu.VMEM((16, CHUNK, 128), F32),
            pltpu.VMEM((CHUNK, 128), F32),
            pltpu.VMEM((8, CHUNK, 128), F32),
            sem(16), sem(16), sem(16), sem(16), sem(8), sem(8), sem(16), sem(16), sem(16), sem(16),
        ],
        compiler_params=pltpu.CompilerParams(collective_id=1, has_side_effects=True, vmem_limit_bytes=VMEM_LIMIT),
        name="total_over_devices",
    )(payload.reshape(2, 16, CHUNK, 128))


def brick_codes(occupancy):
    flags = occupancy.reshape(occupancy.shape[0], BX, 16) > 0
    ids = jnp.arange(16, dtype=I32)
    first = jnp.min(jnp.where(flags, ids, NONE), axis=-1)
    last = jnp.max(jnp.where(flags, ids, -1), axis=-1)
    return jnp.stack([first, jnp.where(last > first, last, NONE)], axis=-1)


def unpack(payload, taps, rows):
    return payload.reshape(taps, rows // 2, 2, 64).transpose(0, 2, 1, 3).reshape(taps * rows, 64)


def per_device(feats, occupancy, assign, w_first, w_second, grad_out):
    tile = lax.axis_index("tile")
    tile_ids = jnp.arange(SCENES, dtype=I32)
    hits = (assign[0][:, None] == tile_ids[None, :]).astype(I32)
    order = jnp.sum(hits * tile_ids[:, None], axis=0)
    codes = brick_codes(occupancy)
    at_row = lax.dynamic_index_in_dim(codes, tile // 4, 1, keepdims=False)
    code = jnp.sum(hits[:, :, None] * at_row[:, None, :], axis=0).reshape(SCENES * SLOTS)
    own_hit = (assign[0] == tile).astype(I32)
    own_code = jnp.sum(own_hit[:, None] * codes.reshape(SCENES, NB), axis=0)
    bricks = relayout(pack(order, code, feats))
    w3 = w_second.reshape(27, 64, 64)[::-1].transpose(0, 2, 1).reshape(27 * 64, 64)
    decoded, payload = scene_step(own_code, bricks, w_first, w_second, w3, grad_out[0])
    factor = 1.0 / math.sqrt(256 * 16 * 16 * 16)
    total = total_over_devices(payload, factor).reshape(32 * CHUNK, 128)
    grad_first = unpack(total[0:432], 9, 96)
    grad_second = unpack(total[432:1296], 9, 192)
    return decoded[None], grad_first, grad_second


def solution(mesh):
    return jax.shard_map(
        per_device,
        mesh=mesh,
        in_specs=(
            P("scene", "tile", None, None),
            P("scene", None, None, None),
            P("scene", None),
            P(),
            P(),
            P(("scene", "tile"), None, None, None),
        ),
        out_specs=(P(("scene", "tile"), None, None, None), P(), P()),
        check_vma=False,
    )
```

time: 483 us -> 79.1 us (0.16); the launches traced: 476 us -> 78.7 us
  waiting for transfers between devices: 310 us -> 0 us
  matrix products: 70.6 us -> 0 us
  Pallas kernels: 0 us -> 61.2 us
  local copies, waits for them, and re-layouts: 43.5 us -> 13 us
  starting transfers between devices: 20.1 us -> 0 us
  between operations: 16.9 us -> 0.75 us
  other arithmetic: 14.4 us -> 3.8 us
    psum x1 -> x0, waiting for transfers between devices: 254 us -> none  [per_device(): lax.psum((part_first, part_second), ('scene', 'tile'))]
    conv_general_dilated x5 -> x0, matrix products: 70.6 us -> none  [the longest x2 40.3 us: kernel_grad(): lax.conv_general_dilated(lhs, rhs, (1, 1, 1), 'VALID', rhs_dilation=(dila...]
    pallas_call x0 -> x4, Pallas kernels: none -> 61.2 us  [the longest x1 33.9 us: total_over_devices(): pl.pallas_call(functools.partial(total_kernel, factor), out_shape=jax.Sha...]
    ppermute x1 -> x0, waiting for transfers between devices: 45.4 us -> none  [shifted(): lax.ppermute(value, axis, [(source, source + steps) for source in range(f...]
    reshape x7, local copies, waits for them, and re-layouts: 20.7 us -> 5.35 us  [the longest x5 4.18 us: unpack(): payload.reshape(taps, rows // 2, 2, 64).transpose(0, 2, 1, 3)]
    all_to_all x2 -> x0, starting transfers between devices: 15.1 us -> none  [the longest x1 10.9 us: per_device(): lax.all_to_all(outgoing, 'tile', split_axis=0, concat_axis=1, tiled=True)]
    all_to_all x2 -> x0, waiting for transfers between devices: 10.6 us -> none  [the longest x1 10.6 us: per_device(): lax.all_to_all(outgoing, 'tile', split_axis=0, concat_axis=1, tiled=True)]
    mul x3 -> x0, other arithmetic: 9.5 us -> none  [the longest x1 8.19 us: per_device(): feats.reshape(local_scenes, planes, wide_y, depth, c_full)]
  transfers between devices with their start and end apart: 4 -> 0, of which waited for: 3 -> 0; matrix products, arithmetic and copies ran while one was open for 8% -> 0% of each run, Pallas kernels for 0% -> 0%
where the time goes in v1:
time: 79.1 us; the launch traced here: 78.7 us
  Pallas kernels  61.2 us (77%)
  local copies, waits for them, and re-layouts  13 us (16%)
  other arithmetic  3.8 us (5%)
    pallas_call x1, Pallas kernels, total_over_devices(): pl.pallas_call(functools.partial(total_kernel, factor), out_shape=jax.Sha...  33.9 us
    pallas_call x1, Pallas kernels, relayout(): pl.pallas_call(relayout_kernel, out_shape=jax.ShapeDtypeStruct((SCENES, 3...  17.7 us
    pallas_call x1, Pallas kernels, scene_step(): pl.pallas_call(scene_kernel, out_shape=[jax.ShapeDtypeStruct((16, 16, 102...  6.74 us
    reshape x5, local copies, waits for them, and re-layouts, unpack(): payload.reshape(taps, rows // 2, 2, 64).transpose(0, 2, 1, 3)  4.18 us
    pallas_call x1, Pallas kernels, pack(): pl.pallas_call(pack_kernel, out_shape=jax.ShapeDtypeStruct((SCENES, 32, 2...  2.82 us
    unnamed x4, local copies, waits for them, and re-layouts  2.7 us

profile of v1, /device:TPU:1, one launch (start us, length us, event | category | flops | bytes accessed | tf_op | source)
XLA Modules:
  0.0 78.7 jit_solution(11827357754818777837)
XLA Ops:
  0.6 0.0 copy-start
  0.7 0.7 compare_convert_fusion
  1.4 1.2 %select_reduce_fusion.2.order_ref = s32[16]{0:T(128)} fusion(s32[16]{0:T(128)} %bitcast.32), kind=kLoop, calls=%fused_computation.4 | loop fusion | flops 752 | bytes 128 | tf_op jit(solution)/shard_map/reduce_sum | solution.py:428
  2.6 0.9 %select_reduce_fusion.1 = (s32[16,4]{0,1:T(4,128)S(1)}, s32[16,4]{0,1:T(4,128)S(1)}) fusion(s32[4,4]{1,0:T(4,128)S(1)} %multiply_add_fusion, s32[16,4,4,4]{0,3,2,1:T(4,128)} %param.7), kind=kLoop, calls=%fused_computation.1 | loop fusion | flops 4992 | bytes 4672 | tf_op jit(solution)/shard_map/reduce_min | solution.py:415
  3.5 0.1 fusion.2
  3.7 0.1 copy.33
  3.8 0.7 reduce_sum.30.code_ref
  4.4 0.7 fusion
  5.1 0.1 multiply_reduce_fusion
  5.2 0.1 copy.34
  5.3 0.7 reshape.88.code_ref
  6.0 1.7 %copy.36.w1_ref = bf16[864,64]{1,0:T(8,128)(2,1)} copy(bf16[864,64]{0,1:T(8,128)(2,1)} %param.9) | data formatting | bytes 221184 | tf_op args[3]
  7.7 2.8 %pack.1.stage = bf16[16,32,256]{2,1,0:T(8,128)(2,1)} custom-call(s32[16]{0:T(128)} %select_reduce_fusion.2.order_ref, s32[32]{0:T(128)} %reshape.88.code_ref, bf16[16,2,32,1024]{3,2,1,0:T(8,128)(2,1)} %feats_ref.1), custom_call_target="tpu_custom_call" | custom-call | tf_op jit(solution)/shard_map/pack/pallas_call | solution.py:47
  10.5 17.7 %relayout.1.bricks_ref = bf16[16,32,256]{2,1,0:T(8,128)(2,1)} custom-call(bf16[16,32,256]{2,1,0:T(8,128)(2,1)} %pack.1.stage), custom_call_target="tpu_custom_call" | custom-call | tf_op jit(solution)/shard_map/relayout/pallas_call | solution.py:85
  28.3 0.0 copy-done
  28.3 1.0 %copy.37.w2_ref = bf16[1728,64]{1,0:T(8,128)(2,1)} copy(bf16[1728,64]{0,1:T(8,128)(2,1)S(1)} %copy-done) | data formatting | bytes 442368 | tf_op args[4]
  29.3 0.5 reshape.89
  29.7 0.5 rev.3
  30.3 0.9 %copy.35 = bf16[27,64,64]{2,1,0:T(8,128)(2,1)} copy(bf16[27,64,64]{2,0,1:T(8,128)(2,1)S(1)} %bitcast.25) | data formatting | bytes 442368 | tf_op jit(solution)/shard_map/transpose | solution.py:435
  31.2 6.7 %scene_step.1 = (bf16[16,16,1024]{2,1,0:T(8,128)(2,1)}, f32[1536,128]{1,0:T(8,128)}) custom-call(s32[8]{0:T(128)} %reduce_sum.30.code_ref, bf16[16,32,256]{2,1,0:T(8,128)(2,1)} %relayout.1.bricks_ref, bf16[864,64]{1,0:T(8,128)(2,1)} %copy.36.w1_ref, bf16[1728,64]{1,0:T(8,128)(2,1)} %copy.37.w2_ref, bf16[1728,64]{1,0:T(8,128)(2,1)} %bitcast.26, ...), custom_call_target="tpu_custom_call" | custom-call | tf_op jit(solution)/shard_map/scene_step/pallas_call | solution.py:273
  37.9 33.9 %total_over_devices.1 = f32[2,16,48,128]{3,2,1,0:T(8,128)} custom-call(f32[2,16,48,128]{3,2,1,0:T(8,128)} %bitcast.27), custom_call_target="tpu_custom_call" | custom-call | tf_op jit(solution)/shard_map/total_over_devices/pallas_call | solution.py:394
  71.9 1.0 %slice.8 = f32[432,128]{1,0:T(8,128)S(1)} slice(f32[1536,128]{1,0:T(8,128)} %bitcast.22), slice={[0:432], [0:128]} | slice | bytes 442368 | tf_op jit(solution)/shard_map/slice | solution.py:439
  72.8 1.0 %slice.9 = f32[864,128]{1,0:T(8,128)S(1)} slice(f32[1536,128]{1,0:T(8,128)} %bitcast.23), slice={[432:1296], [0:128]} | slice | bytes 884736 | tf_op jit(solution)/shard_map/slice | solution.py:440
  73.9 0.3 reshape.93
  74.1 1.0 %copy.38 = f32[9,48,2,64]{1,2,0,3:T(2,128)S(1)} copy(f32[9,48,2,64]{3,2,1,0:T(2,128)S(1)} %reshape.93) | data formatting | bytes 442368 | tf_op jit(solution)/shard_map/reshape | solution.py:421
  75.2 1.1 %reshape.94 = f32[864,64]{0,1:T(8,128)} reshape(f32[9,2,48,64]{2,1,0,3:T(2,128)S(1)} %bitcast.24) | data formatting | bytes 442368 | tf_op jit(solution)/shard_map/reshape | solution.py:421
  76.3 0.5 reshape.95
  76.8 0.6 copy.39
  77.5 1.2 %reshape.96 = f32[1728,64]{0,1:T(8,128)} reshape(f32[9,2,96,64]{2,1,0,3:T(2,128)S(1)} %copy.39) | data formatting | bytes 884736 | tf_op jit(solution)/shard_map/reshape | solution.py:421
  (3 shorter events, 0.0 us)
Async XLA Ops:
  0.6 27.6 %copy-start = (bf16[1728,64]{0,1:T(8,128)(2,1)S(1)}, bf16[1728,64]{0,1:T(8,128)(2,1)}, u32[]{:S(2)}) copy-start(bf16[1728,64]{0,1:T(8,128)(2,1)} %param.10) | copy-start | bytes 663556

commit v2 on v1

--- a/solution.py
+++ b/solution.py
@@ -25,46 +25,61 @@
     return pl.BlockSpec(memory_space=pltpu.SMEM)
 
 
-def pack_kernel(order_ref, code_ref, feats_ref, out_ref):
-    @pl.loop(0, SCENES)
-    def _(target):
-        scene = order_ref[target]
-        rows = []
-        for slot in range(SLOTS):
-            code = code_ref[target * SLOTS + slot]
-            by = code // 4
-            bz = code - 4 * by
-            for plane in range(2):
-                wide = feats_ref[scene, plane, :, pl.ds(pl.multiple_of(bz * 256, 256), 256)].astype(F32)
-                acc = jnp.zeros((8, 256), F32)
-                for k in range(4):
-                    acc = jnp.where(by == k, wide[8 * k : 8 * k + 8], acc)
-                rows.append(acc)
-        out_ref[target] = jnp.concatenate(rows, axis=0).astype(BF16)
-
-
-def pack(order, code, feats):
-    return pl.pallas_call(
-        pack_kernel,
-        out_shape=jax.ShapeDtypeStruct((SCENES, 32, 256), BF16),
-        in_specs=[smem(), smem(), vmem()],
-        out_specs=vmem(),
-        compiler_params=pltpu.CompilerParams(vmem_limit_bytes=VMEM_LIMIT),
-        name="pack",
-    )(order, code, feats)
-
-
-def relayout_kernel(stage, out_ref, send_sem, recv_sem):
+def iota(shape, dim):
+    return lax.broadcasted_iota(I32, shape, dim)
+
+
+def row_codes(planes):
+    first, last = NONE, -1
+    for by in range(4):
+        flags = planes[by] > 0
+        ids = iota(planes[by].shape, 0) + 4 * by
+        first = jnp.minimum(first, jnp.where(flags, ids, NONE))
+        last = jnp.maximum(last, jnp.where(flags, ids, -1))
+    first = jnp.min(first.astype(F32), axis=0, keepdims=True).astype(I32)
+    last = jnp.max(last.astype(F32), axis=0, keepdims=True).astype(I32)
+    return first, jnp.where(last > first, last, NONE)
+
+
+def relayout_kernel(assign_ref, owner_ref, occ_ref, feats_ref, out_ref, own_ref, packed, stage, send_sem, recv_sem):
     me = lax.axis_index("tile")
     barrier = pltpu.get_barrier_semaphore()
     for step in range(1, SCENES):
         peer = lax.rem(me + step, SCENES)
         pl.semaphore_signal(barrier, inc=1, device_id={"tile": peer}, device_id_type=MESH)
-    out_ref[me] = stage[me]
+
+    here = me // 4
+    slots = row_codes([occ_ref[here, by] for by in range(4)])
+    for scene in range(SCENES):
+        marks = [jnp.broadcast_to(code[:, scene : scene + 1], (8, 256)) for code in slots]
+        bys = [mark // 4 for mark in marks]
+        bzs = [mark % 4 for mark in marks]
+        rows = [[None, None], [None, None]]
+        for plane in range(2):
+            wide = feats_ref[scene, plane].astype(F32)
+            for slot in range(SLOTS):
+                acc = jnp.zeros((8, 256), F32)
+                for by in range(4):
+                    line = wide[8 * by : 8 * by + 8]
+                    part = line[:, 0:256]
+                    for bz in range(1, 4):
+                        part = jnp.where(bzs[slot] == bz, line[:, 256 * bz : 256 * bz + 256], part)
+                    acc = jnp.where(bys[slot] == by, part, acc)
+                rows[slot][plane] = acc
+        packed[scene] = jnp.concatenate(rows[0] + rows[1], axis=0).astype(BF16)
+
+    def scene_of(target):
+        scene = 0
+        for j in range(SCENES):
+            scene = jnp.where(assign_ref[0, j] == target, j, scene)
+        return scene
+
+    out_ref[me] = packed[scene_of(me)]
     pl.semaphore_wait(barrier, SCENES - 1)
     copies = []
     for step in range(1, SCENES):
         peer = lax.rem(me + step, SCENES)
+        stage[peer] = packed[scene_of(peer)]
         copy = pltpu.make_async_remote_copy(
             src_ref=stage.at[peer],
             dst_ref=out_ref.at[me],
@@ -75,29 +90,36 @@
         )
         copy.start()
         copies.append(copy)
+    codes = []
+    for bx in range(BX):
+        codes += row_codes([occ_ref[bx, by] for by in range(4)])
+    mine = jnp.where(owner_ref[...] == me, jnp.concatenate(codes, axis=0), 0)
+    own = jnp.sum(mine.astype(F32), axis=1, keepdims=True).astype(I32)
+    own_ref[...] = jnp.broadcast_to(own, (NB, 128))
     for copy in copies:
         copy.wait_recv()
     for copy in copies:
         copy.wait_send()
 
 
-def relayout(stage):
+def relayout(assign, occupancy, feats):
     return pl.pallas_call(
         relayout_kernel,
-        out_shape=jax.ShapeDtypeStruct((SCENES, 32, 256), BF16),
-        in_specs=[vmem()],
-        out_specs=vmem(),
+        out_shape=[
+            jax.ShapeDtypeStruct((SCENES, 32, 256), BF16),
+            jax.ShapeDtypeStruct((NB, 128), I32),
+        ],
+        in_specs=[smem(), vmem(), vmem(), vmem()],
+        out_specs=[vmem(), vmem()],
         scratch_shapes=[
+            pltpu.VMEM((SCENES, 32, 256), BF16),
+            pltpu.VMEM((SCENES, 32, 256), BF16),
             pltpu.SemaphoreType.DMA((SCENES,)),
             pltpu.SemaphoreType.DMA((SCENES,)),
         ],
         compiler_params=pltpu.CompilerParams(collective_id=0, has_side_effects=True, vmem_limit_bytes=VMEM_LIMIT),
         name="relayout",
-    )(stage)
-
-
-def iota(shape, dim):
-    return lax.broadcasted_iota(I32, shape, dim)
+    )(assign, assign, occupancy.transpose(1, 2, 3, 0), feats)
 
 
 def dot(lhs, rhs, dims=((1,), (0,))):
@@ -113,9 +135,9 @@
     return pieces[0] if len(pieces) == 1 else jnp.concatenate(pieces, axis=1)
 
 
-def scene_kernel(code_ref, bricks_ref, w1_ref, w2_ref, w3_ref, cot_ref, dec_ref, pay_ref,
+def scene_kernel(code_ref, bricks_ref, w1_ref, w2_ref, cot_ref, dec_ref, pay_ref,
                  fe, he, de, wide1, wide2, wide3, p1, p2, p3):
-    codes = [code_ref[b] for b in range(NB)]
+    codes = [code_ref[b, 0] for b in range(NB)]
     valid = [code < NONE for code in codes]
     bys = [code // 4 for code in codes]
     bzs = [code - 4 * by for code, by in zip(codes, bys)]
@@ -145,22 +167,26 @@
     wide1[...] = jnp.zeros_like(wide1)
     wide2[...] = jnp.zeros_like(wide2)
     wide3[...] = jnp.zeros_like(wide3)
+    def turned(ref):
+        return ref[...].astype(F32).T.astype(BF16)
+
+    first, second = turned(w1_ref), turned(w2_ref)
     for tap in range(9):
         base = tap * 384
-        w = w1_ref[tap * 96 : tap * 96 + 96, :]
+        w = first[tap * 96 : tap * 96 + 96]
         wide1[base + 352 : base + 384, 0:64] = w[0:32]
         wide1[base : base + 64, 0:64] = w[32:96]
         for zo in range(1, 4):
             at = base + 32 * (2 * zo - 1)
             wide1[at : at + 96, 64 * zo : 64 * zo + 64] = w
-        for source, target in ((w2_ref, wide2), (w3_ref, wide3)):
-            w = source[tap * 192 : tap * 192 + 192, :]
-            target[base + 320 : base + 384, 0:64] = w[0:64]
-            target[base : base + 128, 0:64] = w[64:192]
-            target[base : base + 192, 64:128] = w
-            target[base + 64 : base + 256, 128:192] = w
-            target[base + 128 : base + 256, 192:256] = w[0:128]
-            target[base + 256 : base + 320, 192:256] = w[128:192]
+        forward = [second[(3 * tap + kz) * 64 : (3 * tap + kz) * 64 + 64] for kz in range(3)]
+        backward = [w2_ref[:, (26 - 3 * tap - kz) * 64 : (26 - 3 * tap - kz) * 64 + 64] for kz in range(3)]
+        for target, blocks in ((wide2, forward), (wide3, backward)):
+            for zo in range(4):
+                for kz in range(3):
+                    zi = zo + kz - 1
+                    at = base + (320 if zi < 0 else 64 * zi)
+                    target[at : at + 64, 64 * zo : 64 * zo + 64] = blocks[kz]
 
     row, col = iota((128, 128), 0), iota((128, 128), 1)
     source = ((row // 2) % 4) * 32 + (row % 2) * 16 + (row // 64) * 8 + (row // 8) % 8
@@ -241,33 +267,42 @@
     d_hidden = dot(p3[...], wide3[...]).astype(BF16)
     d_pre = (d_hidden.astype(F32) * (sig_pre * (1.0 + pre * (1.0 - sig_pre)))).astype(BF16)
 
-    def fold(parts, target):
-        half = parts[0].shape[0] // 2
+    def halves(parts):
+        size = parts[0].shape[0] // 2
         lo, hi = parts[0] + parts[2], parts[1] + parts[3]
-        is_low = iota((half, 128), 1) < 64
-        keep = jnp.where(is_low, lo[:half], hi[half:])
-        turn = jnp.where(is_low, lo[half:], hi[:half])
-        pay_ref[target : target + half, :] = keep + pltpu.roll(turn, 64, 1)
-
+        return [(lo[:size], hi[:size]), (lo[size:], hi[size:])]
+
+    def fold(lower, upper, target):
+        size = lower[0].shape[0]
+        is_low = iota((size, 128), 1) < 64
+        keep = jnp.where(is_low, lower[0], upper[1])
+        turn = jnp.where(is_low, upper[0], lower[1])
+        pay_ref[target : target + size, :] = keep + pltpu.roll(turn, 64, 1)
+
+    blocks1, blocks2 = [], []
+    for tap in range(9):
+        full = dot(p2[:, tap * 384 : tap * 384 + 384], d_second, ((0,), (0,)))
+        blocks2 += halves([
+            jnp.concatenate([full[320:384, 0:128], full[0:128, 0:128]], axis=0),
+            full[0:192, 0:128],
+            full[64:256, 128:256],
+            full[128:320, 128:256],
+        ])
+    for at in range(9):
+        fold(blocks2[at], blocks2[at + 9], 432 + at * 96)
     for tap in range(9):
         full = dot(p1[:, tap * 384 : tap * 384 + 384], d_pre, ((0,), (0,)))
         parts = [jnp.concatenate([full[352:384, 0:128], full[0:64, 0:128]], axis=0)]
         for zo in range(1, 4):
             at, lane = 32 * (2 * zo - 1), 128 * (zo // 2)
             parts.append(full[at : at + 96, lane : lane + 128])
-        fold(parts, tap * 48)
-        full = dot(p2[:, tap * 384 : tap * 384 + 384], d_second, ((0,), (0,)))
-        parts = [
-            jnp.concatenate([full[320:384, 0:128], full[0:128, 0:128]], axis=0),
-            full[0:192, 0:128],
-            full[64:256, 128:256],
-            full[128:320, 128:256],
-        ]
-        fold(parts, 432 + tap * 96)
+        blocks1 += halves(parts)
+    for at in range(9):
+        fold(blocks1[at], blocks1[at + 9], at * 48)
     pay_ref[1296:1536, :] = jnp.zeros((240, 128), F32)
 
 
-def scene_step(code, bricks, w1, w2, w3, cot):
+def scene_step(code, bricks, w1, w2, cot):
     wide = pltpu.VMEM((3456, 256), BF16)
     patch = pltpu.VMEM((128, 3456), BF16)
     return pl.pallas_call(
@@ -276,7 +311,7 @@
             jax.ShapeDtypeStruct((16, 16, 1024), BF16),
             jax.ShapeDtypeStruct((32 * CHUNK, 128), F32),
         ],
-        in_specs=[smem()] + [vmem()] * 5,
+        in_specs=[smem()] + [vmem()] * 4,
         out_specs=[vmem(), vmem()],
         scratch_shapes=[
             pltpu.VMEM((9, 9, 8, 384), F32),
@@ -286,7 +321,7 @@
         ],
         compiler_params=pltpu.CompilerParams(vmem_limit_bytes=VMEM_LIMIT),
         name="scene_step",
-    )(code, bricks, w1, w2, w3, cot)
+    )(code, bricks, w1, w2, cot)
 
 
 def total_kernel(factor, pay_ref, out_ref, from_core, mine, from_scene, part, from_z,
@@ -335,9 +370,9 @@
         cores[step].wait_recv()
         added = pay_ref[core, owner] + from_core[owner]
         if step == 0:
-            from_scene[scene] = added
+            from_scene[scene] = added.astype(BF16)
             continue
-        mine[owner] = added
+        mine[owner] = added.astype(BF16)
         copy = remote(
             mine.at[owner], from_scene.at[scene], scene_send.at[step], scene_recv.at[step], to_scene(owner)
         )
@@ -346,11 +381,11 @@
     waits += scenes
     for copy in scenes:
         copy.wait_recv()
-    total = from_scene[0]
+    total = from_scene[0].astype(F32)
     for k in range(1, 16):
-        total = total + from_scene[k]
-    part[...] = total
-    from_z[z] = total
+        total = total + from_scene[k].astype(F32)
+    part[...] = total.astype(BF16)
+    from_z[z] = total.astype(BF16)
     zs = []
     for step in range(1, 8):
         copy = remote(
@@ -361,10 +396,10 @@
     waits += zs
     for copy in zs:
         copy.wait_recv()
-    total = from_z[0]
+    total = from_z[0].astype(F32)
     for k in range(1, 8):
-        total = total + from_z[k]
-    out_ref[core, scene] = total * factor
+        total = total + from_z[k].astype(F32)
+    out_ref[core, scene] = (total * factor).astype(BF16)
     outs = [None]
     backs = []
     for step in range(1, 16):
@@ -393,15 +428,15 @@
     sem = lambda n: pltpu.SemaphoreType.DMA((n,))
     return pl.pallas_call(
         functools.partial(total_kernel, factor),
-        out_shape=jax.ShapeDtypeStruct((2, 16, CHUNK, 128), F32),
+        out_shape=jax.ShapeDtypeStruct((2, 16, CHUNK, 128), BF16),
         in_specs=[vmem()],
         out_specs=vmem(),
         scratch_shapes=[
             pltpu.VMEM((16, CHUNK, 128), F32),
-            pltpu.VMEM((16, CHUNK, 128), F32),
-            pltpu.VMEM((16, CHUNK, 128), F32),
-            pltpu.VMEM((CHUNK, 128), F32),
-            pltpu.VMEM((8, CHUNK, 128), F32),
+            pltpu.VMEM((16, CHUNK, 128), BF16),
+            pltpu.VMEM((16, CHUNK, 128), BF16),
+            pltpu.VMEM((CHUNK, 128), BF16),
+            pltpu.VMEM((8, CHUNK, 128), BF16),
             sem(16), sem(16), sem(16), sem(16), sem(8), sem(8), sem(16), sem(16), sem(16), sem(16),
         ],
         compiler_params=pltpu.CompilerParams(collective_id=1, has_side_effects=True, vmem_limit_bytes=VMEM_LIMIT),
@@ -409,36 +444,32 @@
     )(payload.reshape(2, 16, CHUNK, 128))
 
 
-def brick_codes(occupancy):
-    flags = occupancy.reshape(occupancy.shape[0], BX, 16) > 0
-    ids = jnp.arange(16, dtype=I32)
-    first = jnp.min(jnp.where(flags, ids, NONE), axis=-1)
-    last = jnp.max(jnp.where(flags, ids, -1), axis=-1)
-    return jnp.stack([first, jnp.where(last > first, last, NONE)], axis=-1)
-
-
-def unpack(payload, taps, rows):
-    return payload.reshape(taps, rows // 2, 2, 64).transpose(0, 2, 1, 3).reshape(taps * rows, 64)
+def unpack_kernel(total_ref, first_ref, second_ref):
+    row, col = iota((64, 128), 0), iota((64, 128), 1)
+    for half in range(2):
+        pick = jnp.where(col == row + 64 * half, 1.0, 0.0).astype(BF16)
+        first_ref[:, 432 * half : 432 * half + 432] = dot(pick, total_ref[0:432], ((1,), (1,)))
+        second_ref[:, 864 * half : 864 * half + 864] = dot(pick, total_ref[432:1296], ((1,), (1,)))
+
+
+def unpack(total):
+    return pl.pallas_call(
+        unpack_kernel,
+        out_shape=[jax.ShapeDtypeStruct((64, 864), F32), jax.ShapeDtypeStruct((64, 1728), F32)],
+        in_specs=[vmem()],
+        out_specs=[vmem(), vmem()],
+        compiler_params=pltpu.CompilerParams(vmem_limit_bytes=VMEM_LIMIT),
+        name="unpack",
+    )(total)
 
 
 def per_device(feats, occupancy, assign, w_first, w_second, grad_out):
-    tile = lax.axis_index("tile")
-    tile_ids = jnp.arange(SCENES, dtype=I32)
-    hits = (assign[0][:, None] == tile_ids[None, :]).astype(I32)
-    order = jnp.sum(hits * tile_ids[:, None], axis=0)
-    codes = brick_codes(occupancy)
-    at_row = lax.dynamic_index_in_dim(codes, tile // 4, 1, keepdims=False)
-    code = jnp.sum(hits[:, :, None] * at_row[:, None, :], axis=0).reshape(SCENES * SLOTS)
-    own_hit = (assign[0] == tile).astype(I32)
-    own_code = jnp.sum(own_hit[:, None] * codes.reshape(SCENES, NB), axis=0)
-    bricks = relayout(pack(order, code, feats))
-    w3 = w_second.reshape(27, 64, 64)[::-1].transpose(0, 2, 1).reshape(27 * 64, 64)
-    decoded, payload = scene_step(own_code, bricks, w_first, w_second, w3, grad_out[0])
+    bricks, own_code = relayout(assign, occupancy, feats)
+    decoded, payload = scene_step(own_code, bricks, w_first.T, w_second.T, grad_out[0])
     factor = 1.0 / math.sqrt(256 * 16 * 16 * 16)
-    total = total_over_devices(payload, factor).reshape(32 * CHUNK, 128)
-    grad_first = unpack(total[0:432], 9, 96)
-    grad_second = unpack(total[432:1296], 9, 192)
-    return decoded[None], grad_first, grad_second
+    total = total_over_devices(payload, factor)
+    grad_first, grad_second = unpack(total.reshape(32 * CHUNK, 128))
+    return decoded[None], grad_first.T, grad_second.T
 
 
 def solution(mesh):

time: 79.1 us -> 56.9 us (0.72)
  local copies, waits for them, and re-layouts: 13 us -> 0 us
  Pallas kernels: 61.2 us -> 56 us
  other arithmetic: 3.8 us -> 0 us
    reshape x7 -> x0, local copies, waits for them, and re-layouts: 5.35 us -> none  [the longest x5 4.18 us: unpack(): payload.reshape(taps, rows // 2, 2, 64).transpose(0, 2, 1, 3)]
    pallas_call x1, Pallas kernels: 33.9 us -> 28.7 us  [total_over_devices(): pl.pallas_call(functools.partial(total_kernel, factor), out_shape=jax.Sha...]
    unnamed x4 -> x0, local copies, waits for them, and re-layouts: 2.7 us -> none
    slice x2 -> x0, local copies, waits for them, and re-layouts: 2 us -> none  [the longest x1 1.04 us: per_device(): grad_second = unpack(total[432:1296], 9, 192)]
    transpose x2 -> x0, local copies, waits for them, and re-layouts: 1.55 us -> none  [the longest x1 0.93 us: per_device(): w_second.reshape(27, 64, 64)[::-1].transpose(0, 2, 1).reshape(27 * 64, 64)]
    reduce_sum x3 -> x0, other arithmetic: 1.48 us -> none  [the longest x1 1.25 us: per_device(): order = jnp.sum(hits * tile_ids[:, None], axis=0)]
    convert_element_type x2 -> x0, other arithmetic: 1.43 us -> none  [the longest x1 0.73 us: per_device(): hits = (assign[0][:, None] == tile_ids[None, :]).astype(I32)]
    reduce_min x1 -> x0, other arithmetic: 0.86 us -> none  [brick_codes(): first = jnp.min(jnp.where(flags, ids, NONE), axis=-1)]
where the time goes in v2:
time: 56.9 us; the launch traced here: 56.7 us
  Pallas kernels  56 us (98%)
  between operations  0.65 us (1%)
    pallas_call x1, Pallas kernels, total_over_devices(): pl.pallas_call(functools.partial(total_kernel, factor), out_shape=jax.Sha...  28.7 us
    pallas_call x1, Pallas kernels, relayout(): pl.pallas_call(relayout_kernel, out_shape=[jax.ShapeDtypeStruct((SCENES,...  18.6 us
    pallas_call x1, Pallas kernels, scene_step(): pl.pallas_call(scene_kernel, out_shape=[jax.ShapeDtypeStruct((16, 16, 102...  6.54 us
    pallas_call x1, Pallas kernels, unpack(): pl.pallas_call(unpack_kernel, out_shape=[jax.ShapeDtypeStruct((64, 864),...  2.2 us

profile of v2, /device:TPU:1, one launch (start us, length us, event | category | flops | bytes accessed | tf_op | source)
XLA Modules:
  0.0 56.7 jit_solution(1991136666156039000)
XLA Ops:
  0.6 18.6 %relayout.1 = (bf16[16,32,256]{2,1,0:T(8,128)(2,1)}, s32[8,128]{1,0:T(8,128)}) custom-call(s32[1,16]{1,0:T(1,128)} %owner_ref.1, s32[1,16]{1,0:T(1,128)} %owner_ref.1, s32[4,4,4,16]{3,2,1,0:T(4,128)} %bitcast.14, bf16[16,2,32,1024]{3,2,1,0:T(8,128)(2,1)} %feats_ref.1), custom_call_target="tpu_custom_call" | custom-call | tf_op jit(solution)/shard_map/relayout/pallas_call | solution.py:106
  19.2 6.5 %scene_step.1 = (bf16[16,16,1024]{2,1,0:T(8,128)(2,1)}, f32[1536,128]{1,0:T(8,128)}) custom-call(s32[8,128]{1,0:T(8,128)} %get-tuple-element.9.code_ref, bf16[16,32,256]{2,1,0:T(8,128)(2,1)} %get-tuple-element.10.bricks_ref, bf16[64,864]{1,0:T(8,128)(2,1)} %bitcast.13, bf16[64,1728]{1,0:T(8,128)(2,1)} %bitcast.12, bf16[16,16,1024]{2,1,0:T(8,128)(2,1)} %bitcast.11), custom_call_target="tpu_custom_call" | custom-call | tf_op jit(solution)/shard_map/scene_step/pallas_call | solution.py:308
  25.7 28.7 %total_over_devices.1 = bf16[2,16,48,128]{3,2,1,0:T(8,128)(2,1)} custom-call(f32[2,16,48,128]{3,2,1,0:T(8,128)} %bitcast.10), custom_call_target="tpu_custom_call" | custom-call | tf_op jit(solution)/shard_map/total_over_devices/pallas_call | solution.py:429
  54.5 2.2 %unpack.1 = (f32[64,864]{1,0:T(8,128)}, f32[64,1728]{1,0:T(8,128)}) custom-call(bf16[1536,128]{1,0:T(8,128)(2,1)} %bitcast.9), custom_call_target="tpu_custom_call" | custom-call | tf_op jit(solution)/shard_map/unpack/pallas_call | solution.py:456

commit v3 on v2

v3 whole, which is shorter than its diff:
```python
import functools
import math

import jax
import jax.numpy as jnp
from jax import lax
from jax.experimental import pallas as pl
from jax.experimental.pallas import tpu as pltpu
from jax.sharding import PartitionSpec as P

MESH = pl.DeviceIdType.MESH
F32, BF16, I32 = jnp.float32, jnp.bfloat16, jnp.int32
SCENES, BX, SLOTS, NB = 16, 4, 2, 8
NONE = 16
TAPS = [(kx, ky) for kx in range(3) for ky in range(3)]
CHUNK = 48
VMEM_LIMIT = 60 * 1024 * 1024


def vmem():
    return pl.BlockSpec(memory_space=pltpu.VMEM)


def smem():
    return pl.BlockSpec(memory_space=pltpu.SMEM)


def iota(shape, dim):
    return lax.broadcasted_iota(I32, shape, dim)


def dot(lhs, rhs, dims=((1,), (0,))):
    return lax.dot_general(lhs, rhs, (dims, ((), ())), preferred_element_type=F32)


def remote(src, dst, send, recv, device):
    return pltpu.make_async_remote_copy(
        src_ref=src, dst_ref=dst, send_sem=send, recv_sem=recv, device_id=device, device_id_type=MESH
    )


def row_codes(planes):
    first, last = NONE, -1
    for by in range(4):
        flags = planes[by] > 0
        ids = iota(planes[by].shape, 0) + 4 * by
        first = jnp.minimum(first, jnp.where(flags, ids, NONE))
        last = jnp.maximum(last, jnp.where(flags, ids, -1))
    first = jnp.min(first.astype(F32), axis=0, keepdims=True).astype(I32)
    last = jnp.max(last.astype(F32), axis=0, keepdims=True).astype(I32)
    return first, jnp.where(last > first, last, NONE)


def pack_scene(feats_ref, scene, slots, packed):
    marks = [jnp.broadcast_to(code[:, scene : scene + 1], (8, 256)) for code in slots]
    bys = [mark // 4 for mark in marks]
    bzs = [mark % 4 for mark in marks]
    rows = [[None, None], [None, None]]
    for plane in range(2):
        wide = feats_ref[scene, plane].astype(F32)
        for slot in range(SLOTS):
            acc = jnp.zeros((8, 256), F32)
            for by in range(4):
                line = wide[8 * by : 8 * by + 8]
                part = line[:, 0:256]
                for bz in range(1, 4):
                    part = jnp.where(bzs[slot] == bz, line[:, 256 * bz : 256 * bz + 256], part)
                acc = jnp.where(bys[slot] == by, part, acc)
            rows[slot][plane] = acc
    packed[scene] = jnp.concatenate(rows[0] + rows[1], axis=0).astype(BF16)


def scene_of(assign_ref, target):
    scene = 0
    for j in range(SCENES):
        scene = jnp.where(assign_ref[0, j] == target, j, scene)
    return scene


def own_codes(occ_ref, owner, me):
    codes = []
    for bx in range(BX):
        codes += row_codes([occ_ref[bx, by] for by in range(4)])
    mine = jnp.where(owner == me, jnp.concatenate(codes, axis=0), 0)
    own = jnp.sum(mine.astype(F32), axis=1, keepdims=True).astype(I32)
    return jnp.broadcast_to(own, (NB, 128))


def sublane_gather(value, picker):
    index, hit = picker
    pieces = []
    for at in range(0, value.shape[1], 128):
        got = jnp.take_along_axis(value[:, at : at + 128], index, axis=0)
        pieces.append(jnp.where(hit, got, 0.0))
    return pieces[0] if len(pieces) == 1 else jnp.concatenate(pieces, axis=1)


def pickers(own):
    sub = iota((NB, 128), 0)
    place = jnp.where(own < NONE, (sub // 2) * 64 + (own // 4) * 8 + own % 4, -10000 * (sub + 1))
    each = [jnp.broadcast_to(place[b : b + 1], (NB, 128)) for b in range(NB)]
    pick = {}
    for dx in (-1, 0, 1):
        for dy in (-1, 0, 1):
            for dz in (-1, 0, 1):
                if (dx, dy, dz) == (0, 0, 0):
                    continue
                target = place + (dx * 64 + dy * 8 + dz)
                index = jnp.zeros((NB, 128), I32)
                hit = jnp.zeros((NB, 128), I32)
                for b in range(NB):
                    same = target == each[b]
                    index = jnp.where(same, b, index)
                    hit = jnp.where(same, 1, hit)
                pick[dx, dy, dz] = index, hit > 0
    return pick


def banded(w1_ref, w2_ref, wide1, wide2, wide3):
    wide1[...] = jnp.zeros_like(wide1)
    wide2[...] = jnp.zeros_like(wide2)
    wide3[...] = jnp.zeros_like(wide3)

    def turned(ref):
        return ref[...].astype(F32).T.astype(BF16)

    first, second = turned(w1_ref), turned(w2_ref)
    for tap in range(9):
        base = tap * 384
        w = first[tap * 96 : tap * 96 + 96]
        wide1[base + 352 : base + 384, 0:64] = w[0:32]
        wide1[base : base + 64, 0:64] = w[32:96]
        for zo in range(1, 4):
            at = base + 32 * (2 * zo - 1)
            wide1[at : at + 96, 64 * zo : 64 * zo + 64] = w
        forward = [second[(3 * tap + kz) * 64 : (3 * tap + kz) * 64 + 64] for kz in range(3)]
        backward = [w2_ref[:, (26 - 3 * tap - kz) * 64 : (26 - 3 * tap - kz) * 64 + 64] for kz in range(3)]
        for target, blocks in ((wide2, forward), (wide3, backward)):
            for zo in range(4):
                for kz in range(3):
                    zi = zo + kz - 1
                    at = base + (320 if zi < 0 else 64 * zi)
                    target[at : at + 64, 64 * zo : 64 * zo + 64] = blocks[kz]


def upstream_bricks(own, cot_ref):
    row, col = iota((32, 128), 0), iota((32, 128), 1)
    start = jnp.where(own < NONE, iota((NB, 128), 0) * 16 + (own // 4) * 4, -10000)
    goal = jnp.concatenate([start] * 4, axis=0) + row // 8
    take = jnp.where(col == goal, 1.0, 0.0).astype(BF16)
    bzs = own % 4
    marks = [jnp.broadcast_to(bzs[b : b + 1, 0:1], (16, 256)) for b in range(NB)]
    ups = []
    for x in range(4):
        planes = []
        for bx in range(BX):
            wide = cot_ref[4 * bx + x].astype(F32)
            for slot in range(SLOTS):
                part = wide[:, 0:256]
                for bz in range(1, 4):
                    part = jnp.where(marks[2 * bx + slot] == bz, wide[:, 256 * bz : 256 * bz + 256], part)
                planes.append(part)
        ups.append(dot(take, jnp.concatenate(planes, axis=0).astype(BF16)))
    return jnp.concatenate(ups, axis=0)


def first_patches(pick, bricks_ref, fe, p1):
    row, col = iota((128, 128), 0), iota((128, 128), 1)
    source = ((row // 2) % 4) * 32 + (row % 2) * 16 + (row // 64) * 8 + (row // 8) % 8
    perm = jnp.where(col == source, 1.0, 0.0).astype(BF16)
    for j in range(4):
        stack = jnp.concatenate([bricks_ref[4 * bx + j] for bx in range(BX)], axis=0)
        moved = dot(perm, stack).reshape(2, 8, 8, 256)
        for plane in range(2):
            fe[2 * j + plane + 1, 1:9, :, 0:256] = moved[plane]
    for px in range(-1, 8):
        for py in range(-1, 8):
            dx, dy = (-1 if px < 0 else 0), (-1 if py < 0 else 0)
            tile = fe[px % 8 + 1, py % 8 + 1, :, 0:256]
            if dx or dy:
                fe[px + 1, py + 1, :, 0:256] = sublane_gather(tile, pick[dx, dy, 0])
            fe[px + 1, py + 1, :, 256:384] = sublane_gather(tile[:, 128:256], pick[dx, dy, -1])
    for tap, (kx, ky) in enumerate(TAPS):
        rows = [fe[2 * x + kx, 2 * y + ky] for x in range(4) for y in range(4)]
        p1[:, tap * 384 : tap * 384 + 384] = jnp.concatenate(rows, axis=0).astype(BF16)


def half_patches(pick, value, ext, patches):
    low = iota((NB, 128), 1) < 64
    for px in range(-1, 5):
        for py in range(-1, 5):
            dx = -1 if px < 0 else (1 if px > 3 else 0)
            dy = -1 if py < 0 else (1 if py > 3 else 0)
            at = ((px % 4) * 4 + py % 4) * 8
            tile = value[at : at + 8]
            if dx or dy:
                ext[px + 1, py + 1, :, 0:256] = sublane_gather(tile, pick[dx, dy, 0])
            else:
                ext[px + 1, py + 1, :, 0:256] = tile
            above = sublane_gather(tile[:, 0:128], pick[dx, dy, 1])
            below = sublane_gather(tile[:, 128:256], pick[dx, dy, -1])
            ext[px + 1, py + 1, :, 256:384] = jnp.where(low, above, below)
    for tap, (kx, ky) in enumerate(TAPS):
        rows = [ext[x + kx, y + ky] for x in range(4) for y in range(4)]
        patches[:, tap * 384 : tap * 384 + 384] = jnp.concatenate(rows, axis=0).astype(BF16)


def halves(parts):
    size = parts[0].shape[0] // 2
    lo, hi = parts[0] + parts[2], parts[1] + parts[3]
    return [(lo[:size], hi[:size]), (lo[size:], hi[size:])]


def fold(pay, lower, upper, target):
    size = lower[0].shape[0]
    is_low = iota((size, 128), 1) < 64
    keep = jnp.where(is_low, lower[0], upper[1])
    turn = jnp.where(is_low, upper[0], lower[1])
    pay[target : target + size, :] = keep + pltpu.roll(turn, 64, 1)


def second_grad(p2, d_second, pay):
    blocks = []
    for tap in range(9):
        full = dot(p2[:, tap * 384 : tap * 384 + 384], d_second, ((0,), (0,)))
        blocks += halves([
            jnp.concatenate([full[320:384, 0:128], full[0:128, 0:128]], axis=0),
            full[0:192, 0:128],
            full[64:256, 128:256],
            full[128:320, 128:256],
        ])
    for at in range(9):
        fold(pay, blocks[at], blocks[at + 9], 432 + at * 96)


def first_grad(p1, d_pre, pay):
    blocks = []
    for tap in range(9):
        full = dot(p1[:, tap * 384 : tap * 384 + 384], d_pre, ((0,), (0,)))
        parts = [jnp.concatenate([full[352:384, 0:128], full[0:64, 0:128]], axis=0)]
        for zo in range(1, 4):
            at, lane = 32 * (2 * zo - 1), 128 * (zo // 2)
            parts.append(full[at : at + 96, lane : lane + 128])
        blocks += halves(parts)
    for at in range(9):
        fold(pay, blocks[at], blocks[at + 9], at * 48)


def scene_step(pick, upstream, bricks_ref, dec_ref, pay, fe, he, de, wide1, wide2, wide3, p1, p2, p3):
    first_patches(pick, bricks_ref, fe, p1)
    pre = dot(p1[...], wide1[...])
    sig_pre = jax.nn.sigmoid(pre)
    hidden = (pre * sig_pre).astype(BF16)
    half_patches(pick, hidden.astype(F32), he, p2)
    second = dot(p2[...], wide2[...])
    sig = jax.nn.sigmoid(second)
    dec_ref[...] = (second * sig).astype(BF16)
    d_second = (upstream * (sig * (1.0 + second * (1.0 - sig)))).astype(BF16)
    second_grad(p2, d_second, pay)
    half_patches(pick, d_second.astype(F32), de, p3)
    d_hidden = dot(p3[...], wide3[...]).astype(BF16)
    d_pre = (d_hidden.astype(F32) * (sig_pre * (1.0 + pre * (1.0 - sig_pre)))).astype(BF16)
    first_grad(p1, d_pre, pay)
    pay[1296:1536, :] = jnp.zeros((240, 128), F32)


def train_kernel(factor, assign_ref, owner_ref, occ_ref, feats_hbm, w1_hbm, w2_hbm, cot_hbm,
                 out_ref, dec_ref, own_ref,
                 feats, w1, w2, cot, packed, stage, bricks,
                 fe, he, de, wide1, wide2, wide3, p1, p2, p3, pay,
                 from_core, mine, from_scene, part, from_z,
                 load_sem, send_sem, recv_sem,
                 core_send, core_recv, scene_send, scene_recv, z_send, z_recv,
                 out_send, out_recv, back_send, back_recv):
    tile, scene = lax.axis_index("tile"), lax.axis_index("scene")
    core = lax.rem(tile, 2)
    z = tile // 2
    sibling = 2 * z + 1 - core
    loads = []
    for at in range(4):
        loads.append(pltpu.make_async_copy(
            feats_hbm.at[pl.ds(4 * at, 4)], feats.at[pl.ds(4 * at, 4)], load_sem.at[at]))
    for at, (src, dst) in enumerate(((w1_hbm, w1), (w2_hbm, w2), (cot_hbm, cot))):
        loads.append(pltpu.make_async_copy(src, dst, load_sem.at[4 + at]))
    for load in loads:
        load.start()
    barrier = pltpu.get_barrier_semaphore()
    for step in range(1, 16):
        pl.semaphore_signal(barrier, inc=1, device_id={"tile": lax.rem(tile + step, 16)}, device_id_type=MESH)
        pl.semaphore_signal(barrier, inc=1, device_id={"scene": lax.rem(scene + step, 16)}, device_id_type=MESH)

    slots = row_codes([occ_ref[tile // 4, by] for by in range(4)])
    for j in range(SCENES):
        if j % 4 == 0:
            loads[j // 4].wait()
        pack_scene(feats, j, slots, packed)
    bricks[tile] = packed[scene_of(assign_ref, tile)]
    pl.semaphore_wait(barrier, 30)
    sends = []
    for step in range(1, SCENES):
        peer = lax.rem(tile + step, SCENES)
        stage[peer] = packed[scene_of(assign_ref, peer)]
        copy = remote(stage.at[peer], bricks.at[tile], send_sem.at[step], recv_sem.at[step], {"tile": peer})
        copy.start()
        sends.append(copy)

    own = own_codes(occ_ref, owner_ref[...], tile)
    own_ref[...] = own
    loads[4].wait()
    loads[5].wait()
    banded(w1, w2, wide1, wide2, wide3)
    pick = pickers(own)
    loads[6].wait()
    upstream = upstream_bricks(own, cot)
    for copy in sends:
        copy.wait_recv()

    scene_step(pick, upstream, bricks, dec_ref, pay, fe, he, de, wide1, wide2, wide3, p1, p2, p3)

    def rows(half, owner):
        return pl.ds(pl.multiple_of((half * 16 + owner) * CHUNK, CHUNK), CHUNK)

    waits = list(sends)
    cores = []
    for step in range(16):
        owner = lax.rem(scene + step, 16)
        copy = remote(
            pay.at[rows(1 - core, owner)], from_core.at[owner], core_send.at[step], core_recv.at[step],
            {"tile": sibling},
        )
        copy.start()
        cores.append(copy)
    waits += cores
    scenes = []
    for step in list(range(1, 16)) + [0]:
        owner = lax.rem(scene + step, 16)
        cores[step].wait_recv()
        added = (pay[rows(core, owner)] + from_core[owner]).astype(BF16)
        if step == 0:
            from_scene[scene] = added
            continue
        mine[owner] = added
        copy = remote(
            mine.at[owner], from_scene.at[scene], scene_send.at[step], scene_recv.at[step], {"scene": owner}
        )
        copy.start()
        scenes.append(copy)
    waits += scenes
    for copy in scenes:
        copy.wait_recv()
    total = from_scene[0].astype(F32)
    for k in range(1, 16):
        total = total + from_scene[k].astype(F32)
    part[...] = total.astype(BF16)
    from_z[z] = total.astype(BF16)
    zs = []
    for step in range(1, 8):
        peer = lax.rem(z + step, 8)
        copy = remote(part, from_z.at[z], z_send.at[step], z_recv.at[step], {"tile": 2 * peer + core})
        copy.start()
        zs.append(copy)
    waits += zs
    for copy in zs:
        copy.wait_recv()
    total = from_z[0].astype(F32)
    for k in range(1, 8):
        total = total + from_z[k].astype(F32)
    out_ref[rows(core, scene)] = (total * factor).astype(BF16)
    outs = [None]
    backs = []
    for step in range(1, 16):
        here = out_ref.at[rows(core, scene)]
        copy = remote(here, here, out_send.at[step], out_recv.at[step], {"scene": lax.rem(scene + step, 16)})
        copy.start()
        outs.append(copy)
    waits += outs[1:]
    for step in range(16):
        if step:
            outs[step].wait_recv()
        here = out_ref.at[rows(core, lax.rem(scene - step + 16, 16))]
        copy = remote(here, here, back_send.at[step], back_recv.at[step], {"tile": sibling})
        copy.start()
        backs.append(copy)
    waits += backs
    for copy in backs:
        copy.wait_recv()
    for copy in waits:
        copy.wait_send()


def compute_scratch():
    wide = pltpu.VMEM((3456, 256), BF16)
    patch = pltpu.VMEM((128, 3456), BF16)
    return [
        pltpu.VMEM((9, 9, 8, 384), F32),
        pltpu.VMEM((6, 6, 8, 384), F32),
        pltpu.VMEM((6, 6, 8, 384), F32),
        wide, wide, wide, patch, patch, patch,
    ]


def train(assign, occupancy, feats, w1, w2, cot, factor):
    sem = lambda n: pltpu.SemaphoreType.DMA((n,))
    chunk = lambda n, dtype: pltpu.VMEM((n, CHUNK, 128), dtype)
    anyspace = pl.BlockSpec(memory_space=pl.ANY)
    return pl.pallas_call(
        functools.partial(train_kernel, factor),
        out_shape=[
            jax.ShapeDtypeStruct((32 * CHUNK, 128), BF16),
            jax.ShapeDtypeStruct((128, 256), BF16),
            jax.ShapeDtypeStruct((NB, 128), I32),
        ],
        in_specs=[smem(), vmem(), vmem()] + [anyspace] * 4,
        out_specs=[vmem()] * 3,
        scratch_shapes=[
            pltpu.VMEM(feats.shape, BF16),
            pltpu.VMEM(w1.shape, BF16),
            pltpu.VMEM(w2.shape, BF16),
            pltpu.VMEM(cot.shape, BF16),
            pltpu.VMEM((SCENES, 32, 256), BF16),
            pltpu.VMEM((SCENES, 32, 256), BF16),
            pltpu.VMEM((SCENES, 32, 256), BF16),
            *compute_scratch(),
            pltpu.VMEM((32 * CHUNK, 128), F32),
            chunk(16, F32), chunk(16, BF16), chunk(16, BF16),
            pltpu.VMEM((CHUNK, 128), BF16),
            chunk(8, BF16),
            sem(7), sem(16), sem(16),
            sem(16), sem(16), sem(16), sem(16), sem(8), sem(8), sem(16), sem(16), sem(16), sem(16),
        ],
        compiler_params=pltpu.CompilerParams(collective_id=0, has_side_effects=True, vmem_limit_bytes=VMEM_LIMIT),
        name="train",
    )(assign, assign, occupancy.transpose(1, 2, 3, 0), feats, w1, w2, cot)


def unpack_kernel(code_ref, total_ref, compact_ref, first_ref, second_ref, dec_ref):
    row, col = iota((64, 128), 0), iota((64, 128), 1)
    for half in range(2):
        pick = jnp.where(col == row + 64 * half, 1.0, 0.0).astype(BF16)
        first_ref[:, 432 * half : 432 * half + 432] = dot(pick, total_ref[0:432], ((1,), (1,)))
        second_ref[:, 864 * half : 864 * half + 864] = dot(pick, total_ref[432:1296], ((1,), (1,)))
    codes = [code_ref[b, 0] for b in range(NB)]
    bys = [code // 4 for code in codes]
    bzs = [code - 4 * by for code, by in zip(codes, bys)]
    row, col = iota((128, 32), 0), iota((128, 32), 1)
    goal = jnp.full((128, 32), -1, I32)
    for b in range(NB):
        start = jnp.where(codes[b] < NONE, 16 * b + 4 * bys[b], -10000)
        goal = jnp.where(col % 8 == b, start + col // 8, goal)
    give = jnp.where(row == goal, 1.0, 0.0).astype(BF16)
    for x in range(4):
        spread = dot(give, compact_ref[32 * x : 32 * x + 32])
        for bx in range(BX):
            one, two = spread[32 * bx : 32 * bx + 16], spread[32 * bx + 16 : 32 * bx + 32]
            for c in range(4):
                block = jnp.where(bzs[2 * bx] == c, one, 0.0) + jnp.where(bzs[2 * bx + 1] == c, two, 0.0)
                dec_ref[4 * bx + x, :, 256 * c : 256 * c + 256] = block.astype(BF16)


def unpack(code, total, compact):
    return pl.pallas_call(
        unpack_kernel,
        out_shape=[
            jax.ShapeDtypeStruct((64, 864), F32),
            jax.ShapeDtypeStruct((64, 1728), F32),
            jax.ShapeDtypeStruct((16, 16, 1024), BF16),
        ],
        in_specs=[smem(), vmem(), vmem()],
        out_specs=[vmem()] * 3,
        compiler_params=pltpu.CompilerParams(vmem_limit_bytes=VMEM_LIMIT),
        name="unpack",
    )(code, total, compact)


def per_device(feats, occupancy, assign, w_first, w_second, grad_out):
    factor = 1.0 / math.sqrt(256 * 16 * 16 * 16)
    total, compact, code = train(assign, occupancy, feats, w_first.T, w_second.T, grad_out[0], factor)
    grad_first, grad_second, decoded = unpack(code, total, compact)
    return decoded[None], grad_first.T, grad_second.T


def solution(mesh):
    return jax.shard_map(
        per_device,
        mesh=mesh,
        in_specs=(
            P("scene", "tile", None, None),
            P("scene", None, None, None),
            P("scene", None),
            P(),
            P(),
            P(("scene", "tile"), None, None, None),
        ),
        out_specs=(P(("scene", "tile"), None, None, None), P(), P()),
        check_vma=False,
    )
```

time: 56.9 us -> 47.4 us (0.83)
  Pallas kernels: 56 us -> 46.6 us
    pallas_call x3 -> x1, Pallas kernels: 53.8 us -> 44.1 us  [train(): pl.pallas_call(functools.partial(train_kernel, factor), out_shape=[jax.Sh...]
where the time goes in v3:
time: 47.4 us; the launch traced here: 47.2 us
  Pallas kernels  46.6 us (98%)
  between operations  0.64 us (1%)
    pallas_call x1, Pallas kernels, train(): pl.pallas_call(functools.partial(train_kernel, factor), out_shape=[jax.Sh...  44.1 us
    pallas_call x1, Pallas kernels, unpack(): pl.pallas_call(unpack_kernel, out_shape=[jax.ShapeDtypeStruct((64, 864),...  2.45 us

profile of v3, /device:TPU:1, one launch (start us, length us, event | category | flops | bytes accessed | tf_op | source)
XLA Modules:
  0.0 47.2 jit_solution(15969024681635775571)
XLA Ops:
  0.6 44.1 %train.1 = (bf16[1536,128]{1,0:T(8,128)(2,1)}, bf16[128,256]{1,0:T(8,128)(2,1)}, s32[8,128]{1,0:T(8,128)}) custom-call(s32[1,16]{1,0:T(1,128)} %owner_ref.1, s32[1,16]{1,0:T(1,128)} %owner_ref.1, s32[4,4,4,16]{3,2,1,0:T(4,128)} %bitcast.10, bf16[16,2,32,1024]{3,2,1,0:T(8,128)(2,1)} %feats_hbm.1, bf16[64,864]{1,0:T(8,128)(2,1)} %bitcast.9, ...), custom_call_target="tpu_custom_call" | custom-call | tf_op jit(solution)/shard_map/train/pallas_call | solution.py:406
  44.8 2.5 %unpack.1 = (f32[64,864]{1,0:T(8,128)}, f32[64,1728]{1,0:T(8,128)}, bf16[16,16,1024]{2,1,0:T(8,128)(2,1)}) custom-call(s32[8,128]{1,0:T(8,128)} %get-tuple-element.9.code_ref, bf16[1536,128]{1,0:T(8,128)(2,1)} %get-tuple-element.10.total_ref, bf16[128,256]{1,0:T(8,128)(2,1)} %get-tuple-element.11.compact_ref), custom_call_target="tpu_custom_call" | custom-call | tf_op jit(solution)/shard_map/unpack/pallas_call | solution.py:461

commit v4 on v3

--- a/solution.py
+++ b/solution.py
@@ -13,8 +13,8 @@
 SCENES, BX, SLOTS, NB = 16, 4, 2, 8
 NONE = 16
 TAPS = [(kx, ky) for kx in range(3) for ky in range(3)]
-CHUNK = 48
-VMEM_LIMIT = 60 * 1024 * 1024
+SECOND_ROWS, FIRST_ROWS = 32, 16
+VMEM_LIMIT = 40 * 1024 * 1024
 
 
 def vmem():
@@ -230,7 +230,7 @@
             full[128:320, 128:256],
         ])
     for at in range(9):
-        fold(pay, blocks[at], blocks[at + 9], 432 + at * 96)
+        fold(pay, blocks[at], blocks[at + 9], at * 96)
 
 
 def first_grad(p1, d_pre, pay):
@@ -246,7 +246,7 @@
         fold(pay, blocks[at], blocks[at + 9], at * 48)
 
 
-def scene_step(pick, upstream, bricks_ref, dec_ref, pay, fe, he, de, wide1, wide2, wide3, p1, p2, p3):
+def forward(pick, upstream, bricks_ref, dec_ref, pay2, fe, he, wide1, wide2, p1, p2):
     first_patches(pick, bricks_ref, fe, p1)
     pre = dot(p1[...], wide1[...])
     sig_pre = jax.nn.sigmoid(pre)
@@ -256,43 +256,137 @@
     sig = jax.nn.sigmoid(second)
     dec_ref[...] = (second * sig).astype(BF16)
     d_second = (upstream * (sig * (1.0 + second * (1.0 - sig)))).astype(BF16)
-    second_grad(p2, d_second, pay)
+    second_grad(p2, d_second, pay2)
+    return sig_pre * (1.0 + pre * (1.0 - sig_pre)), d_second
+
+
+def hidden_grad(pick, slope, d_second, de, wide3, p3):
     half_patches(pick, d_second.astype(F32), de, p3)
     d_hidden = dot(p3[...], wide3[...]).astype(BF16)
-    d_pre = (d_hidden.astype(F32) * (sig_pre * (1.0 + pre * (1.0 - sig_pre)))).astype(BF16)
-    first_grad(p1, d_pre, pay)
-    pay[1296:1536, :] = jnp.zeros((240, 128), F32)
-
-
-def train_kernel(factor, assign_ref, owner_ref, occ_ref, feats_hbm, w1_hbm, w2_hbm, cot_hbm,
-                 out_ref, dec_ref, own_ref,
-                 feats, w1, w2, cot, packed, stage, bricks,
-                 fe, he, de, wide1, wide2, wide3, p1, p2, p3, pay,
-                 from_core, mine, from_scene, part, from_z,
-                 load_sem, send_sem, recv_sem,
-                 core_send, core_recv, scene_send, scene_recv, z_send, z_recv,
-                 out_send, out_recv, back_send, back_recv):
+    return (d_hidden.astype(F32) * slope).astype(BF16)
+
+
+class Total:
+    def __init__(self, rows, factor, pay, out, from_core, mine, from_scene, part, from_z, send, recv):
+        self.rows, self.factor = rows, factor
+        self.pay, self.out, self.from_core, self.mine = pay, out, from_core, mine
+        self.from_scene, self.part, self.from_z, self.send, self.recv = from_scene, part, from_z, send, recv
+        tile = lax.axis_index("tile")
+        self.scene, self.core, self.z = lax.axis_index("scene"), lax.rem(tile, 2), tile // 2
+        self.sibling = {"tile": 2 * self.z + 1 - self.core}
+        self.started = []
+
+    def chunk(self, half, owner):
+        return pl.ds(pl.multiple_of((half * 16 + owner) * self.rows, self.rows), self.rows)
+
+    def copy(self, src, dst, kind, step, device):
+        copy = remote(src, dst, self.send.at[kind, step], self.recv.at[kind, step], device)
+        copy.start()
+        self.started.append(copy)
+        return copy
+
+    def owner(self, step):
+        return lax.rem(self.scene + step, 16)
+
+    def to_core(self):
+        self.cores = []
+        for step in range(16):
+            owner = self.owner(step)
+            self.cores.append(self.copy(
+                self.pay.at[self.chunk(1 - self.core, owner)], self.from_core.at[owner], 0, step, self.sibling))
+
+    def to_scene(self):
+        self.scenes = []
+        for step in list(range(1, 16)) + [0]:
+            owner = self.owner(step)
+            self.cores[step].wait_recv()
+            added = (self.pay[self.chunk(self.core, owner)] + self.from_core[owner]).astype(BF16)
+            if step == 0:
+                self.from_scene[self.scene] = added
+                continue
+            self.mine[owner] = added
+            self.scenes.append(self.copy(
+                self.mine.at[owner], self.from_scene.at[self.scene], 1, step, {"scene": owner}))
+
+    def to_z(self):
+        for copy in self.scenes:
+            copy.wait_recv()
+        total = self.from_scene[0].astype(F32)
+        for k in range(1, 16):
+            total = total + self.from_scene[k].astype(F32)
+        self.part[...] = total.astype(BF16)
+        self.from_z[self.z] = total.astype(BF16)
+        self.zs = []
+        for step in range(1, 8):
+            peer = lax.rem(self.z + step, 8)
+            self.zs.append(self.copy(
+                self.part, self.from_z.at[self.z], 2, step, {"tile": 2 * peer + self.core}))
+
+    def to_all(self):
+        for copy in self.zs:
+            copy.wait_recv()
+        total = self.from_z[0].astype(F32)
+        for k in range(1, 8):
+            total = total + self.from_z[k].astype(F32)
+        here = self.out.at[self.chunk(self.core, self.scene)]
+        here[...] = (total * self.factor).astype(BF16)
+        self.outs = [None]
+        for step in range(1, 16):
+            self.outs.append(self.copy(here, here, 3, step, {"scene": self.owner(step)}))
+
+    def back(self):
+        self.backs = []
+        for step in range(16):
+            if step:
+                self.outs[step].wait_recv()
+            here = self.out.at[self.chunk(self.core, lax.rem(self.scene - step + 16, 16))]
+            self.backs.append(self.copy(here, here, 4, step, self.sibling))
+
+    def finish(self):
+        for copy in self.backs:
+            copy.wait_recv()
+        for copy in self.started:
+            copy.wait_send()
+
+
+def total_scratch(rows):
+    chunk = lambda n, dtype: pltpu.VMEM((n, rows, 128), dtype)
+    return [
+        pltpu.VMEM((32 * rows, 128), F32),
+        chunk(16, F32), chunk(16, BF16), chunk(16, BF16),
+        pltpu.VMEM((rows, 128), BF16),
+        chunk(8, BF16),
+        pltpu.SemaphoreType.DMA((5, 16)),
+        pltpu.SemaphoreType.DMA((5, 16)),
+    ]
+
+
+def train_kernel(factor, assign_hbm, occ_hbm, feats_hbm, w1_hbm, w2_hbm, cot_hbm,
+                 out1_ref, out2_ref, dec_ref, own_ref,
+                 assign_ref, owner_ref, occ_ref, feats, w1, w2, cot, packed, stage, bricks,
+                 fe, he, de, wide1, wide2, wide3, p1, p2, p3,
+                 load_sem, send_sem, recv_sem, *totals):
     tile, scene = lax.axis_index("tile"), lax.axis_index("scene")
-    core = lax.rem(tile, 2)
-    z = tile // 2
-    sibling = 2 * z + 1 - core
-    loads = []
-    for at in range(4):
-        loads.append(pltpu.make_async_copy(
-            feats_hbm.at[pl.ds(4 * at, 4)], feats.at[pl.ds(4 * at, 4)], load_sem.at[at]))
-    for at, (src, dst) in enumerate(((w1_hbm, w1), (w2_hbm, w2), (cot_hbm, cot))):
-        loads.append(pltpu.make_async_copy(src, dst, load_sem.at[4 + at]))
+    barrier = pltpu.get_barrier_semaphore()
+    for step in (8, 7, 9, 6, 10, 5, 11, 4, 12, 3, 13, 2, 14, 1, 15):
+        pl.semaphore_signal(barrier, inc=1, device_id={"tile": lax.rem(tile + step, 16)}, device_id_type=MESH)
+        pl.semaphore_signal(barrier, inc=1, device_id={"scene": lax.rem(scene + step, 16)}, device_id_type=MESH)
+    pieces = [(assign_hbm, assign_ref), (assign_hbm, owner_ref), (occ_hbm, occ_ref)]
+    pieces += [(feats_hbm.at[pl.ds(4 * at, 4)], feats.at[pl.ds(4 * at, 4)]) for at in range(4)]
+    pieces += [(w1_hbm, w1), (w2_hbm, w2), (cot_hbm, cot)]
+    loads = [pltpu.make_async_copy(src, dst, load_sem.at[at]) for at, (src, dst) in enumerate(pieces)]
     for load in loads:
         load.start()
-    barrier = pltpu.get_barrier_semaphore()
-    for step in range(1, 16):
-        pl.semaphore_signal(barrier, inc=1, device_id={"tile": lax.rem(tile + step, 16)}, device_id_type=MESH)
-        pl.semaphore_signal(barrier, inc=1, device_id={"scene": lax.rem(scene + step, 16)}, device_id_type=MESH)
-
+    pay1, pay2 = totals[0], totals[8]
+    sum1 = Total(FIRST_ROWS, factor, pay1, out1_ref, *totals[1:8])
+    sum2 = Total(SECOND_ROWS, factor, pay2, out2_ref, *totals[9:16])
+
+    for load in loads[:3]:
+        load.wait()
     slots = row_codes([occ_ref[tile // 4, by] for by in range(4)])
     for j in range(SCENES):
         if j % 4 == 0:
-            loads[j // 4].wait()
+            loads[3 + j // 4].wait()
         pack_scene(feats, j, slots, packed)
     bricks[tile] = packed[scene_of(assign_ref, tile)]
     pl.semaphore_wait(barrier, 30)
@@ -306,85 +400,33 @@
 
     own = own_codes(occ_ref, owner_ref[...], tile)
     own_ref[...] = own
-    loads[4].wait()
-    loads[5].wait()
+    loads[7].wait()
+    loads[8].wait()
     banded(w1, w2, wide1, wide2, wide3)
     pick = pickers(own)
-    loads[6].wait()
+    loads[9].wait()
     upstream = upstream_bricks(own, cot)
+    pay1[432:512, :] = jnp.zeros((80, 128), F32)
+    pay2[864:1024, :] = jnp.zeros((160, 128), F32)
     for copy in sends:
         copy.wait_recv()
 
-    scene_step(pick, upstream, bricks, dec_ref, pay, fe, he, de, wide1, wide2, wide3, p1, p2, p3)
-
-    def rows(half, owner):
-        return pl.ds(pl.multiple_of((half * 16 + owner) * CHUNK, CHUNK), CHUNK)
-
-    waits = list(sends)
-    cores = []
-    for step in range(16):
-        owner = lax.rem(scene + step, 16)
-        copy = remote(
-            pay.at[rows(1 - core, owner)], from_core.at[owner], core_send.at[step], core_recv.at[step],
-            {"tile": sibling},
-        )
-        copy.start()
-        cores.append(copy)
-    waits += cores
-    scenes = []
-    for step in list(range(1, 16)) + [0]:
-        owner = lax.rem(scene + step, 16)
-        cores[step].wait_recv()
-        added = (pay[rows(core, owner)] + from_core[owner]).astype(BF16)
-        if step == 0:
-            from_scene[scene] = added
-            continue
-        mine[owner] = added
-        copy = remote(
-            mine.at[owner], from_scene.at[scene], scene_send.at[step], scene_recv.at[step], {"scene": owner}
-        )
-        copy.start()
-        scenes.append(copy)
-    waits += scenes
-    for copy in scenes:
-        copy.wait_recv()
-    total = from_scene[0].astype(F32)
-    for k in range(1, 16):
-        total = total + from_scene[k].astype(F32)
-    part[...] = total.astype(BF16)
-    from_z[z] = total.astype(BF16)
-    zs = []
-    for step in range(1, 8):
-        peer = lax.rem(z + step, 8)
-        copy = remote(part, from_z.at[z], z_send.at[step], z_recv.at[step], {"tile": 2 * peer + core})
-        copy.start()
-        zs.append(copy)
-    waits += zs
-    for copy in zs:
-        copy.wait_recv()
-    total = from_z[0].astype(F32)
-    for k in range(1, 8):
-        total = total + from_z[k].astype(F32)
-    out_ref[rows(core, scene)] = (total * factor).astype(BF16)
-    outs = [None]
-    backs = []
-    for step in range(1, 16):
-        here = out_ref.at[rows(core, scene)]
-        copy = remote(here, here, out_send.at[step], out_recv.at[step], {"scene": lax.rem(scene + step, 16)})
-        copy.start()
-        outs.append(copy)
-    waits += outs[1:]
-    for step in range(16):
-        if step:
-            outs[step].wait_recv()
-        here = out_ref.at[rows(core, lax.rem(scene - step + 16, 16))]
-        copy = remote(here, here, back_send.at[step], back_recv.at[step], {"tile": sibling})
-        copy.start()
-        backs.append(copy)
-    waits += backs
-    for copy in backs:
-        copy.wait_recv()
-    for copy in waits:
+    slope, d_second = forward(pick, upstream, bricks, dec_ref, pay2, fe, he, wide1, wide2, p1, p2)
+    sum2.to_core()
+    d_pre = hidden_grad(pick, slope, d_second, de, wide3, p3)
+    sum2.to_scene()
+    first_grad(p1, d_pre, pay1)
+    sum1.to_core()
+    sum1.to_scene()
+    sum2.to_z()
+    sum1.to_z()
+    sum2.to_all()
+    sum1.to_all()
+    sum2.back()
+    sum1.back()
+    sum2.finish()
+    sum1.finish()
+    for copy in sends:
         copy.wait_send()
 
 
@@ -401,18 +443,22 @@
 
 def train(assign, occupancy, feats, w1, w2, cot, factor):
     sem = lambda n: pltpu.SemaphoreType.DMA((n,))
-    chunk = lambda n, dtype: pltpu.VMEM((n, CHUNK, 128), dtype)
-    anyspace = pl.BlockSpec(memory_space=pl.ANY)
+    anyspace = pl.BlockSpec(memory_space=pltpu.HBM)
+    planes = occupancy.transpose(1, 2, 3, 0)
     return pl.pallas_call(
         functools.partial(train_kernel, factor),
         out_shape=[
-            jax.ShapeDtypeStruct((32 * CHUNK, 128), BF16),
-            jax.ShapeDtypeStruct((128, 256), BF16),
-            jax.ShapeDtypeStruct((NB, 128), I32),
+            pltpu.VMEM((32 * FIRST_ROWS, 128), BF16),
+            pltpu.VMEM((32 * SECOND_ROWS, 128), BF16),
+            pltpu.VMEM((128, 256), BF16),
+            pltpu.VMEM((NB, 128), I32),
         ],
-        in_specs=[smem(), vmem(), vmem()] + [anyspace] * 4,
-        out_specs=[vmem()] * 3,
+        in_specs=[anyspace] * 6,
+        out_specs=[vmem()] * 4,
         scratch_shapes=[
+            pltpu.SMEM(assign.shape, I32),
+            pltpu.VMEM(assign.shape, I32),
+            pltpu.VMEM(planes.shape, I32),
             pltpu.VMEM(feats.shape, BF16),
             pltpu.VMEM(w1.shape, BF16),
             pltpu.VMEM(w2.shape, BF16),
@@ -421,24 +467,17 @@
             pltpu.VMEM((SCENES, 32, 256), BF16),
             pltpu.VMEM((SCENES, 32, 256), BF16),
             *compute_scratch(),
-            pltpu.VMEM((32 * CHUNK, 128), F32),
-            chunk(16, F32), chunk(16, BF16), chunk(16, BF16),
-            pltpu.VMEM((CHUNK, 128), BF16),
-            chunk(8, BF16),
-            sem(7), sem(16), sem(16),
-            sem(16), sem(16), sem(16), sem(16), sem(8), sem(8), sem(16), sem(16), sem(16), sem(16),
+            sem(10), sem(16), sem(16),
+            *total_scratch(FIRST_ROWS),
+            *total_scratch(SECOND_ROWS),
         ],
         compiler_params=pltpu.CompilerParams(collective_id=0, has_side_effects=True, vmem_limit_bytes=VMEM_LIMIT),
         name="train",
-    )(assign, assign, occupancy.transpose(1, 2, 3, 0), feats, w1, w2, cot)
-
-
-def unpack_kernel(code_ref, total_ref, compact_ref, first_ref, second_ref, dec_ref):
-    row, col = iota((64, 128), 0), iota((64, 128), 1)
-    for half in range(2):
-        pick = jnp.where(col == row + 64 * half, 1.0, 0.0).astype(BF16)
-        first_ref[:, 432 * half : 432 * half + 432] = dot(pick, total_ref[0:432], ((1,), (1,)))
-        second_ref[:, 864 * half : 864 * half + 864] = dot(pick, total_ref[432:1296], ((1,), (1,)))
+    )(*(pltpu.with_memory_space_constraint(x, pltpu.HBM) for x in (assign, planes, feats, w1, w2, cot)))
+
+
+def unpack_kernel(code_ref, total1_ref, total2_ref, compact_ref, first_hbm, second_hbm, dec_hbm,
+                  first_ref, second_ref, dec_ref, sem):
     codes = [code_ref[b, 0] for b in range(NB)]
     bys = [code // 4 for code in codes]
     bzs = [code - 4 * by for code, by in zip(codes, bys)]
@@ -455,9 +494,21 @@
             for c in range(4):
                 block = jnp.where(bzs[2 * bx] == c, one, 0.0) + jnp.where(bzs[2 * bx + 1] == c, two, 0.0)
                 dec_ref[4 * bx + x, :, 256 * c : 256 * c + 256] = block.astype(BF16)
-
-
-def unpack(code, total, compact):
+    stores = [pltpu.make_async_copy(dec_ref, dec_hbm, sem.at[0])]
+    stores[0].start()
+    row, col = iota((64, 128), 0), iota((64, 128), 1)
+    picks = [jnp.where(col == row + 64 * half, 1.0, 0.0).astype(BF16) for half in range(2)]
+    jobs = ((second_ref, second_hbm, total2_ref, 864), (first_ref, first_hbm, total1_ref, 432))
+    for at, (ref, hbm, total_ref, count) in enumerate(jobs):
+        for half in range(2):
+            ref[:, count * half : count * half + count] = dot(picks[half], total_ref[0:count], ((1,), (1,)))
+        stores.append(pltpu.make_async_copy(ref, hbm, sem.at[1 + at]))
+        stores[-1].start()
+    for store in stores:
+        store.wait()
+
+
+def unpack(code, total1, total2, compact):
     return pl.pallas_call(
         unpack_kernel,
         out_shape=[
@@ -465,17 +516,23 @@
             jax.ShapeDtypeStruct((64, 1728), F32),
             jax.ShapeDtypeStruct((16, 16, 1024), BF16),
         ],
-        in_specs=[smem(), vmem(), vmem()],
-        out_specs=[vmem()] * 3,
+        in_specs=[smem(), vmem(), vmem(), vmem()],
+        out_specs=[pl.BlockSpec(memory_space=pl.ANY)] * 3,
+        scratch_shapes=[
+            pltpu.VMEM((64, 864), F32),
+            pltpu.VMEM((64, 1728), F32),
+            pltpu.VMEM((16, 16, 1024), BF16),
+            pltpu.SemaphoreType.DMA((3,)),
+        ],
         compiler_params=pltpu.CompilerParams(vmem_limit_bytes=VMEM_LIMIT),
         name="unpack",
-    )(code, total, compact)
+    )(code, total1, total2, compact)
 
 
 def per_device(feats, occupancy, assign, w_first, w_second, grad_out):
     factor = 1.0 / math.sqrt(256 * 16 * 16 * 16)
-    total, compact, code = train(assign, occupancy, feats, w_first.T, w_second.T, grad_out[0], factor)
-    grad_first, grad_second, decoded = unpack(code, total, compact)
+    total1, total2, compact, code = train(assign, occupancy, feats, w_first.T, w_second.T, grad_out[0], factor)
+    grad_first, grad_second, decoded = unpack(code, total1, total2, compact)
     return decoded[None], grad_first.T, grad_second.T
 
 

time: 47.4 us -> 45.6 us (0.962)
  Pallas kernels: 46.6 us -> 44.8 us
    pallas_call x1, Pallas kernels: 44.1 us -> 42.8 us  [train(): pl.pallas_call(functools.partial(train_kernel, factor), out_shape=[pltpu....]
where the time goes in v4:
time: 45.6 us; the launch traced here: 45.5 us
  Pallas kernels  44.8 us (98%)
  between operations  0.64 us (1%)
    pallas_call x1, Pallas kernels, train(): pl.pallas_call(functools.partial(train_kernel, factor), out_shape=[pltpu....  42.8 us
    pallas_call x1, Pallas kernels, unpack(): pl.pallas_call(unpack_kernel, out_shape=[jax.ShapeDtypeStruct((64, 864),...  1.99 us

profile of v4, /device:TPU:1, one launch (start us, length us, event | category | flops | bytes accessed | tf_op | source)
XLA Modules:
  0.0 45.5 jit_solution(8035048025811867086)
XLA Ops:
  0.6 42.8 %train.1 = (bf16[512,128]{1,0:T(8,128)(2,1)S(1)}, bf16[1024,128]{1,0:T(8,128)(2,1)S(1)}, bf16[128,256]{1,0:T(8,128)(2,1)S(1)}, s32[8,128]{1,0:T(8,128)S(1)}) custom-call(s32[1,16]{1,0:T(1,128)} %assign_hbm.1, s32[4,4,4,16]{3,2,1,0:T(4,128)} %bitcast.10, bf16[16,2,32,1024]{3,2,1,0:T(8,128)(2,1)} %feats_hbm.1, bf16[64,864]{1,0:T(8,128)(2,1)} %bitcast.9, ...), custom_call_target="tpu_custom_call" | custom-call | tf_op jit(solution)/shard_map/train/pallas_call | solution.py:448
  43.5 2.0 %unpack.1 = (f32[64,864]{1,0:T(8,128)}, f32[64,1728]{1,0:T(8,128)}, bf16[16,16,1024]{2,1,0:T(8,128)(2,1)}) custom-call(s32[8,128]{1,0:T(8,128)S(1)} %get-tuple-element.10.code_ref, bf16[512,128]{1,0:T(8,128)(2,1)S(1)} %get-tuple-element.11.total1_ref, bf16[1024,128]{1,0:T(8,128)(2,1)S(1)} %get-tuple-element.12.total2_ref, ...), custom_call_target="tpu_custom_call" | custom-call | tf_op jit(solution)/shard_map/unpack/pallas_call | solution.py:512

commit v5 on v4

--- a/solution.py
+++ b/solution.py
@@ -15,6 +15,7 @@
 TAPS = [(kx, ky) for kx in range(3) for ky in range(3)]
 SECOND_ROWS, FIRST_ROWS = 32, 16
 VMEM_LIMIT = 40 * 1024 * 1024
+FAR_FIRST = (8, 7, 9, 6, 10, 5, 11, 4, 12, 3, 13, 2, 14, 1, 15)
 
 
 def vmem():
@@ -37,6 +38,10 @@
     return pltpu.make_async_remote_copy(
         src_ref=src, dst_ref=dst, send_sem=send, recv_sem=recv, device_id=device, device_id_type=MESH
     )
+
+
+def wait_bytes(ref, sem):
+    pltpu.make_async_copy(ref, ref, sem).wait()
 
 
 def row_codes(planes):
@@ -143,13 +148,16 @@
                     target[at : at + 64, 64 * zo : 64 * zo + 64] = blocks[kz]
 
 
-def upstream_bricks(own, cot_ref):
+def takers(own):
     row, col = iota((32, 128), 0), iota((32, 128), 1)
     start = jnp.where(own < NONE, iota((NB, 128), 0) * 16 + (own // 4) * 4, -10000)
     goal = jnp.concatenate([start] * 4, axis=0) + row // 8
     take = jnp.where(col == goal, 1.0, 0.0).astype(BF16)
     bzs = own % 4
-    marks = [jnp.broadcast_to(bzs[b : b + 1, 0:1], (16, 256)) for b in range(NB)]
+    return take, [jnp.broadcast_to(bzs[b : b + 1, 0:1], (16, 256)) for b in range(NB)]
+
+
+def upstream_bricks(take, marks, cot_ref):
     ups = []
     for x in range(4):
         planes = []
@@ -162,6 +170,16 @@
                 planes.append(part)
         ups.append(dot(take, jnp.concatenate(planes, axis=0).astype(BF16)))
     return jnp.concatenate(ups, axis=0)
+
+
+def spread_bricks(take, marks, compact, dec_ref):
+    for x in range(4):
+        spread = dot(take, compact[32 * x : 32 * x + 32], ((0,), (0,)))
+        for bx in range(BX):
+            one, two = spread[32 * bx : 32 * bx + 16], spread[32 * bx + 16 : 32 * bx + 32]
+            for c in range(4):
+                block = jnp.where(marks[2 * bx] == c, one, 0.0) + jnp.where(marks[2 * bx + 1] == c, two, 0.0)
+                dec_ref[4 * bx + x, :, 256 * c : 256 * c + 256] = block.astype(BF16)
 
 
 def first_patches(pick, bricks_ref, fe, p1):
@@ -246,7 +264,7 @@
         fold(pay, blocks[at], blocks[at + 9], at * 48)
 
 
-def forward(pick, upstream, bricks_ref, dec_ref, pay2, fe, he, wide1, wide2, p1, p2):
+def forward(pick, upstream, bricks_ref, pay2, fe, he, wide1, wide2, p1, p2):
     first_patches(pick, bricks_ref, fe, p1)
     pre = dot(p1[...], wide1[...])
     sig_pre = jax.nn.sigmoid(pre)
@@ -254,10 +272,10 @@
     half_patches(pick, hidden.astype(F32), he, p2)
     second = dot(p2[...], wide2[...])
     sig = jax.nn.sigmoid(second)
-    dec_ref[...] = (second * sig).astype(BF16)
+    decoded = (second * sig).astype(BF16)
     d_second = (upstream * (sig * (1.0 + second * (1.0 - sig)))).astype(BF16)
     second_grad(p2, d_second, pay2)
-    return sig_pre * (1.0 + pre * (1.0 - sig_pre)), d_second
+    return sig_pre * (1.0 + pre * (1.0 - sig_pre)), d_second, decoded
 
 
 def hidden_grad(pick, slope, d_second, de, wide3, p3):
@@ -274,101 +292,92 @@
         tile = lax.axis_index("tile")
         self.scene, self.core, self.z = lax.axis_index("scene"), lax.rem(tile, 2), tile // 2
         self.sibling = {"tile": 2 * self.z + 1 - self.core}
-        self.started = []
 
     def chunk(self, half, owner):
         return pl.ds(pl.multiple_of((half * 16 + owner) * self.rows, self.rows), self.rows)
 
-    def copy(self, src, dst, kind, step, device):
-        copy = remote(src, dst, self.send.at[kind, step], self.recv.at[kind, step], device)
+    def copy(self, src, dst, kind, device):
+        copy = remote(src, dst, self.send.at[kind], self.recv.at[kind], device)
         copy.start()
-        self.started.append(copy)
         return copy
+
+    def half(self, core):
+        size = 16 * self.rows
+        return pl.ds(pl.multiple_of(core * size, size), size)
+
+    def owned(self, owner):
+        return pl.ds(pl.multiple_of(owner * self.rows, self.rows), self.rows)
 
     def owner(self, step):
         return lax.rem(self.scene + step, 16)
 
     def to_core(self):
-        self.cores = []
-        for step in range(16):
+        self.there = self.copy(self.pay.at[self.half(1 - self.core)], self.from_core, 0, self.sibling)
+
+    def to_scene(self):
+        self.there.wait_recv()
+        self.mine[...] = (self.pay[self.half(self.core)] + self.from_core[...]).astype(BF16)
+        for step in FAR_FIRST:
             owner = self.owner(step)
-            self.cores.append(self.copy(
-                self.pay.at[self.chunk(1 - self.core, owner)], self.from_core.at[owner], 0, step, self.sibling))
-
-    def to_scene(self):
-        self.scenes = []
-        for step in list(range(1, 16)) + [0]:
-            owner = self.owner(step)
-            self.cores[step].wait_recv()
-            added = (self.pay[self.chunk(self.core, owner)] + self.from_core[owner]).astype(BF16)
-            if step == 0:
-                self.from_scene[self.scene] = added
-                continue
-            self.mine[owner] = added
-            self.scenes.append(self.copy(
-                self.mine.at[owner], self.from_scene.at[self.scene], 1, step, {"scene": owner}))
+            self.copy(self.mine.at[self.owned(owner)], self.from_scene.at[self.scene], 1, {"scene": owner})
+        self.from_scene[self.scene] = self.mine[self.owned(self.scene)]
 
     def to_z(self):
-        for copy in self.scenes:
-            copy.wait_recv()
+        wait_bytes(self.from_scene.at[pl.ds(0, 15)], self.recv.at[1])
         total = self.from_scene[0].astype(F32)
         for k in range(1, 16):
             total = total + self.from_scene[k].astype(F32)
         self.part[...] = total.astype(BF16)
-        self.from_z[self.z] = total.astype(BF16)
-        self.zs = []
-        for step in range(1, 8):
+        for step in (4, 3, 5, 2, 6, 1, 7):
             peer = lax.rem(self.z + step, 8)
-            self.zs.append(self.copy(
-                self.part, self.from_z.at[self.z], 2, step, {"tile": 2 * peer + self.core}))
+            self.copy(self.part, self.from_z.at[self.z], 2, {"tile": 2 * peer + self.core})
+        self.from_z[self.z] = self.part[...]
 
     def to_all(self):
-        for copy in self.zs:
-            copy.wait_recv()
+        wait_bytes(self.from_z.at[pl.ds(0, 7)], self.recv.at[2])
         total = self.from_z[0].astype(F32)
         for k in range(1, 8):
             total = total + self.from_z[k].astype(F32)
         here = self.out.at[self.chunk(self.core, self.scene)]
         here[...] = (total * self.factor).astype(BF16)
-        self.outs = [None]
-        for step in range(1, 16):
-            self.outs.append(self.copy(here, here, 3, step, {"scene": self.owner(step)}))
+        for step in FAR_FIRST:
+            self.copy(here, here, 3, {"scene": self.owner(step)})
 
     def back(self):
-        self.backs = []
-        for step in range(16):
-            if step:
-                self.outs[step].wait_recv()
-            here = self.out.at[self.chunk(self.core, lax.rem(self.scene - step + 16, 16))]
-            self.backs.append(self.copy(here, here, 4, step, self.sibling))
+        wait_bytes(self.out.at[pl.ds(0, 15 * self.rows)], self.recv.at[3])
+        here = self.out.at[self.half(self.core)]
+        self.home = self.copy(here, here, 4, self.sibling)
 
     def finish(self):
-        for copy in self.backs:
-            copy.wait_recv()
-        for copy in self.started:
-            copy.wait_send()
+        self.home.wait_recv()
+        self.there.wait_send()
+        wait_bytes(self.from_scene.at[pl.ds(0, 15)], self.send.at[1])
+        wait_bytes(self.from_z.at[pl.ds(0, 7)], self.send.at[2])
+        wait_bytes(self.out.at[pl.ds(0, 15 * self.rows)], self.send.at[3])
+        self.home.wait_send()
 
 
 def total_scratch(rows):
-    chunk = lambda n, dtype: pltpu.VMEM((n, rows, 128), dtype)
     return [
         pltpu.VMEM((32 * rows, 128), F32),
-        chunk(16, F32), chunk(16, BF16), chunk(16, BF16),
+        pltpu.VMEM((16 * rows, 128), F32),
+        pltpu.VMEM((16 * rows, 128), BF16),
+        pltpu.VMEM((16, rows, 128), BF16),
         pltpu.VMEM((rows, 128), BF16),
-        chunk(8, BF16),
-        pltpu.SemaphoreType.DMA((5, 16)),
-        pltpu.SemaphoreType.DMA((5, 16)),
+        pltpu.VMEM((8, rows, 128), BF16),
+        pltpu.SemaphoreType.DMA((5,)),
+        pltpu.SemaphoreType.DMA((5,)),
     ]
 
 
 def train_kernel(factor, assign_hbm, occ_hbm, feats_hbm, w1_hbm, w2_hbm, cot_hbm,
-                 out1_ref, out2_ref, dec_ref, own_ref,
+                 out1_ref, out2_ref, dec_ref,
                  assign_ref, owner_ref, occ_ref, feats, w1, w2, cot, packed, stage, bricks,
                  fe, he, de, wide1, wide2, wide3, p1, p2, p3,
                  load_sem, send_sem, recv_sem, *totals):
     tile, scene = lax.axis_index("tile"), lax.axis_index("scene")
     barrier = pltpu.get_barrier_semaphore()
-    for step in (8, 7, 9, 6, 10, 5, 11, 4, 12, 3, 13, 2, 14, 1, 15):
+    for step in FAR_FIRST:
         pl.semaphore_signal(barrier, inc=1, device_id={"tile": lax.rem(tile + step, 16)}, device_id_type=MESH)
         pl.semaphore_signal(barrier, inc=1, device_id={"scene": lax.rem(scene + step, 16)}, device_id_type=MESH)
     pieces = [(assign_hbm, assign_ref), (assign_hbm, owner_ref), (occ_hbm, occ_ref)]
@@ -389,35 +398,34 @@
             loads[3 + j // 4].wait()
         pack_scene(feats, j, slots, packed)
     bricks[tile] = packed[scene_of(assign_ref, tile)]
-    pl.semaphore_wait(barrier, 30)
-    sends = []
-    for step in range(1, SCENES):
+    for step in FAR_FIRST:
         peer = lax.rem(tile + step, SCENES)
         stage[peer] = packed[scene_of(assign_ref, peer)]
-        copy = remote(stage.at[peer], bricks.at[tile], send_sem.at[step], recv_sem.at[step], {"tile": peer})
-        copy.start()
-        sends.append(copy)
+    pl.semaphore_wait(barrier, 30)
+    for step in FAR_FIRST:
+        peer = lax.rem(tile + step, SCENES)
+        remote(stage.at[peer], bricks.at[tile], send_sem, recv_sem, {"tile": peer}).start()
 
     own = own_codes(occ_ref, owner_ref[...], tile)
-    own_ref[...] = own
     loads[7].wait()
     loads[8].wait()
     banded(w1, w2, wide1, wide2, wide3)
     pick = pickers(own)
     loads[9].wait()
-    upstream = upstream_bricks(own, cot)
+    take, marks = takers(own)
+    upstream = upstream_bricks(take, marks, cot)
     pay1[432:512, :] = jnp.zeros((80, 128), F32)
     pay2[864:1024, :] = jnp.zeros((160, 128), F32)
-    for copy in sends:
-        copy.wait_recv()
-
-    slope, d_second = forward(pick, upstream, bricks, dec_ref, pay2, fe, he, wide1, wide2, p1, p2)
+    wait_bytes(bricks.at[pl.ds(0, SCENES - 1)], recv_sem)
+
+    slope, d_second, decoded = forward(pick, upstream, bricks, pay2, fe, he, wide1, wide2, p1, p2)
     sum2.to_core()
     d_pre = hidden_grad(pick, slope, d_second, de, wide3, p3)
     sum2.to_scene()
     first_grad(p1, d_pre, pay1)
     sum1.to_core()
     sum1.to_scene()
+    spread_bricks(take, marks, decoded, dec_ref)
     sum2.to_z()
     sum1.to_z()
     sum2.to_all()
@@ -426,8 +434,7 @@
     sum1.back()
     sum2.finish()
     sum1.finish()
-    for copy in sends:
-        copy.wait_send()
+    wait_bytes(bricks.at[pl.ds(0, SCENES - 1)], send_sem)
 
 
 def compute_scratch():
@@ -450,11 +457,10 @@
         out_shape=[
             pltpu.VMEM((32 * FIRST_ROWS, 128), BF16),
             pltpu.VMEM((32 * SECOND_ROWS, 128), BF16),
-            pltpu.VMEM((128, 256), BF16),
-            pltpu.VMEM((NB, 128), I32),
+            pltpu.VMEM(cot.shape, BF16),
         ],
         in_specs=[anyspace] * 6,
-        out_specs=[vmem()] * 4,
+        out_specs=[vmem()] * 3,
         scratch_shapes=[
             pltpu.SMEM(assign.shape, I32),
             pltpu.VMEM(assign.shape, I32),
@@ -467,7 +473,7 @@
             pltpu.VMEM((SCENES, 32, 256), BF16),
             pltpu.VMEM((SCENES, 32, 256), BF16),
             *compute_scratch(),
-            sem(10), sem(16), sem(16),
+            sem(10), pltpu.SemaphoreType.DMA, pltpu.SemaphoreType.DMA,
             *total_scratch(FIRST_ROWS),
             *total_scratch(SECOND_ROWS),
         ],
@@ -476,24 +482,7 @@
     )(*(pltpu.with_memory_space_constraint(x, pltpu.HBM) for x in (assign, planes, feats, w1, w2, cot)))
 
 
-def unpack_kernel(code_ref, total1_ref, total2_ref, compact_ref, first_hbm, second_hbm, dec_hbm,
-                  first_ref, second_ref, dec_ref, sem):
-    codes = [code_ref[b, 0] for b in range(NB)]
-    bys = [code // 4 for code in codes]
-    bzs = [code - 4 * by for code, by in zip(codes, bys)]
-    row, col = iota((128, 32), 0), iota((128, 32), 1)
-    goal = jnp.full((128, 32), -1, I32)
-    for b in range(NB):
-        start = jnp.where(codes[b] < NONE, 16 * b + 4 * bys[b], -10000)
-        goal = jnp.where(col % 8 == b, start + col // 8, goal)
-    give = jnp.where(row == goal, 1.0, 0.0).astype(BF16)
-    for x in range(4):
-        spread = dot(give, compact_ref[32 * x : 32 * x + 32])
-        for bx in range(BX):
-            one, two = spread[32 * bx : 32 * bx + 16], spread[32 * bx + 16 : 32 * bx + 32]
-            for c in range(4):
-                block = jnp.where(bzs[2 * bx] == c, one, 0.0) + jnp.where(bzs[2 * bx + 1] == c, two, 0.0)
-                dec_ref[4 * bx + x, :, 256 * c : 256 * c + 256] = block.astype(BF16)
+def unpack_kernel(total1_ref, total2_ref, dec_ref, first_hbm, second_hbm, dec_hbm, first_ref, second_ref, sem):
     stores = [pltpu.make_async_copy(dec_ref, dec_hbm, sem.at[0])]
     stores[0].start()
     row, col = iota((64, 128), 0), iota((64, 128), 1)
@@ -508,31 +497,30 @@
         store.wait()
 
 
-def unpack(code, total1, total2, compact):
+def unpack(total1, total2, decoded):
     return pl.pallas_call(
         unpack_kernel,
         out_shape=[
             jax.ShapeDtypeStruct((64, 864), F32),
             jax.ShapeDtypeStruct((64, 1728), F32),
-            jax.ShapeDtypeStruct((16, 16, 1024), BF16),
+            jax.ShapeDtypeStruct(decoded.shape, BF16),
         ],
-        in_specs=[smem(), vmem(), vmem(), vmem()],
+        in_specs=[vmem(), vmem(), pl.BlockSpec(memory_space=pl.ANY)],
         out_specs=[pl.BlockSpec(memory_space=pl.ANY)] * 3,
         scratch_shapes=[
             pltpu.VMEM((64, 864), F32),
             pltpu.VMEM((64, 1728), F32),
-            pltpu.VMEM((16, 16, 1024), BF16),
             pltpu.SemaphoreType.DMA((3,)),
         ],
         compiler_params=pltpu.CompilerParams(vmem_limit_bytes=VMEM_LIMIT),
         name="unpack",
-    )(code, total1, total2, compact)
+    )(total1, total2, decoded)
 
 
 def per_device(feats, occupancy, assign, w_first, w_second, grad_out):
     factor = 1.0 / math.sqrt(256 * 16 * 16 * 16)
-    total1, total2, compact, code = train(assign, occupancy, feats, w_first.T, w_second.T, grad_out[0], factor)
-    grad_first, grad_second, decoded = unpack(code, total1, total2, compact)
+    total1, total2, compact = train(assign, occupancy, feats, w_first.T, w_second.T, grad_out[0], factor)
+    grad_first, grad_second, decoded = unpack(total1, total2, compact)
     return decoded[None], grad_first.T, grad_second.T
 
 

time: 45.6 us -> 41.4 us (0.908)
  Pallas kernels: 44.8 us -> 40.7 us
    pallas_call x1, Pallas kernels: 42.8 us -> 39.4 us  [train(): pl.pallas_call(functools.partial(train_kernel, factor), out_shape=[pltpu....]
    pallas_call x1, Pallas kernels: 1.99 us -> 1.23 us  [unpack(): pl.pallas_call(unpack_kernel, out_shape=[jax.ShapeDtypeStruct((64, 864),...]
where the time goes in v5:
time: 41.4 us; the launch traced here: 41.3 us
  Pallas kernels  40.7 us (98%)
  between operations  0.64 us (2%)
    pallas_call x1, Pallas kernels, train(): pl.pallas_call(functools.partial(train_kernel, factor), out_shape=[pltpu....  39.4 us
    pallas_call x1, Pallas kernels, unpack(): pl.pallas_call(unpack_kernel, out_shape=[jax.ShapeDtypeStruct((64, 864),...  1.23 us

profile of v5, /device:TPU:1, one launch (start us, length us, event | category | flops | bytes accessed | tf_op | source)
XLA Modules:
  0.0 41.3 jit_solution(3979718505353573390)
XLA Ops:
  0.6 39.4 %train.1 = (bf16[512,128]{1,0:T(8,128)(2,1)S(1)}, bf16[1024,128]{1,0:T(8,128)(2,1)S(1)}, bf16[16,16,1024]{2,1,0:T(8,128)(2,1)S(1)}) custom-call(s32[1,16]{1,0:T(1,128)} %assign_hbm.1, s32[4,4,4,16]{3,2,1,0:T(4,128)} %bitcast.10, bf16[16,2,32,1024]{3,2,1,0:T(8,128)(2,1)} %feats_hbm.1, bf16[64,864]{1,0:T(8,128)(2,1)} %bitcast.9, bf16[64,1728]{1,0:T(8,128)(2,1)} %bitcast.8, ...), custom_call_target="tpu_custom_call" | custom-call | tf_op jit(solution)/shard_map/train/pallas_call | solution.py:455
  40.1 1.2 %unpack.1 = (f32[64,864]{1,0:T(8,128)}, f32[64,1728]{1,0:T(8,128)}, bf16[16,16,1024]{2,1,0:T(8,128)(2,1)}) custom-call(bf16[512,128]{1,0:T(8,128)(2,1)S(1)} %get-tuple-element.9.total1_ref, bf16[1024,128]{1,0:T(8,128)(2,1)S(1)} %get-tuple-element.10.total2_ref, bf16[16,16,1024]{2,1,0:T(8,128)(2,1)S(1)} %get-tuple-element.11.dec_ref), custom_call_target="tpu_custom_call" | custom-call | tf_op jit(solution)/shard_map/unpack/pallas_call | solution.py:501

commit v6 on v5

--- a/solution.py
+++ b/solution.py
@@ -15,6 +15,10 @@
 TAPS = [(kx, ky) for kx in range(3) for ky in range(3)]
 SECOND_ROWS, FIRST_ROWS = 32, 16
 VMEM_LIMIT = 40 * 1024 * 1024
+PLANE = sorted(
+    ((dy, dx) for dy in range(4) for dx in range(4) if dy or dx),
+    key=lambda d: -(min(d[0], 4 - d[0]) + min(d[1], 4 - d[1])),
+)
 FAR_FIRST = (8, 7, 9, 6, 10, 5, 11, 4, 12, 3, 13, 2, 14, 1, 15)
 
 
@@ -38,6 +42,10 @@
     return pltpu.make_async_remote_copy(
         src_ref=src, dst_ref=dst, send_sem=send, recv_sem=recv, device_id=device, device_id_type=MESH
     )
+
+
+def plane_peer(scene, place):
+    return lax.rem(scene // 4 + place[0], 4) * 4 + lax.rem(lax.rem(scene, 4) + place[1], 4)
 
 
 def wait_bytes(ref, sem):
@@ -308,17 +316,14 @@
     def owned(self, owner):
         return pl.ds(pl.multiple_of(owner * self.rows, self.rows), self.rows)
 
-    def owner(self, step):
-        return lax.rem(self.scene + step, 16)
-
     def to_core(self):
         self.there = self.copy(self.pay.at[self.half(1 - self.core)], self.from_core, 0, self.sibling)
 
     def to_scene(self):
         self.there.wait_recv()
         self.mine[...] = (self.pay[self.half(self.core)] + self.from_core[...]).astype(BF16)
-        for step in FAR_FIRST:
-            owner = self.owner(step)
+        for place in PLANE:
+            owner = plane_peer(self.scene, place)
             self.copy(self.mine.at[self.owned(owner)], self.from_scene.at[self.scene], 1, {"scene": owner})
         self.from_scene[self.scene] = self.mine[self.owned(self.scene)]
 
@@ -340,8 +345,8 @@
             total = total + self.from_z[k].astype(F32)
         here = self.out.at[self.chunk(self.core, self.scene)]
         here[...] = (total * self.factor).astype(BF16)
-        for step in FAR_FIRST:
-            self.copy(here, here, 3, {"scene": self.owner(step)})
+        for place in PLANE:
+            self.copy(here, here, 3, {"scene": plane_peer(self.scene, place)})
 
     def back(self):
         wait_bytes(self.out.at[pl.ds(0, 15 * self.rows)], self.recv.at[3])
@@ -377,9 +382,9 @@
                  load_sem, send_sem, recv_sem, *totals):
     tile, scene = lax.axis_index("tile"), lax.axis_index("scene")
     barrier = pltpu.get_barrier_semaphore()
-    for step in FAR_FIRST:
+    for step, place in zip(FAR_FIRST, PLANE):
         pl.semaphore_signal(barrier, inc=1, device_id={"tile": lax.rem(tile + step, 16)}, device_id_type=MESH)
-        pl.semaphore_signal(barrier, inc=1, device_id={"scene": lax.rem(scene + step, 16)}, device_id_type=MESH)
+        pl.semaphore_signal(barrier, inc=1, device_id={"scene": plane_peer(scene, place)}, device_id_type=MESH)
     pieces = [(assign_hbm, assign_ref), (assign_hbm, owner_ref), (occ_hbm, occ_ref)]
     pieces += [(feats_hbm.at[pl.ds(4 * at, 4)], feats.at[pl.ds(4 * at, 4)]) for at in range(4)]
     pieces += [(w1_hbm, w1), (w2_hbm, w2), (cot_hbm, cot)]
@@ -421,9 +426,9 @@
     slope, d_second, decoded = forward(pick, upstream, bricks, pay2, fe, he, wide1, wide2, p1, p2)
     sum2.to_core()
     d_pre = hidden_grad(pick, slope, d_second, de, wide3, p3)
-    sum2.to_scene()
     first_grad(p1, d_pre, pay1)
     sum1.to_core()
+    sum2.to_scene()
     sum1.to_scene()
     spread_bricks(take, marks, decoded, dec_ref)
     sum2.to_z()

time: 41.4 us -> 40.7 us (0.983)
  Pallas kernels: 40.7 us -> 39.9 us
    pallas_call x1, Pallas kernels: 39.4 us -> 38.7 us  [train(): pl.pallas_call(functools.partial(train_kernel, factor), out_shape=[pltpu....]
where the time goes in v6:
time: 40.7 us; the launch traced here: 40.6 us
  Pallas kernels  39.9 us (98%)
  between operations  0.64 us (2%)
    pallas_call x1, Pallas kernels, train(): pl.pallas_call(functools.partial(train_kernel, factor), out_shape=[pltpu....  38.7 us
    pallas_call x1, Pallas kernels, unpack(): pl.pallas_call(unpack_kernel, out_shape=[jax.ShapeDtypeStruct((64, 864),...  1.23 us

profile of v6, /device:TPU:1, one launch (start us, length us, event | category | flops | bytes accessed | tf_op | source)
XLA Modules:
  0.0 40.6 jit_solution(5010825453303629451)
XLA Ops:
  0.6 38.7 %train.1 = (bf16[512,128]{1,0:T(8,128)(2,1)S(1)}, bf16[1024,128]{1,0:T(8,128)(2,1)S(1)}, bf16[16,16,1024]{2,1,0:T(8,128)(2,1)S(1)}) custom-call(s32[1,16]{1,0:T(1,128)} %assign_hbm.1, s32[4,4,4,16]{3,2,1,0:T(4,128)} %bitcast.10, bf16[16,2,32,1024]{3,2,1,0:T(8,128)(2,1)} %feats_hbm.1, bf16[64,864]{1,0:T(8,128)(2,1)} %bitcast.9, bf16[64,1728]{1,0:T(8,128)(2,1)} %bitcast.8, ...), custom_call_target="tpu_custom_call" | custom-call | tf_op jit(solution)/shard_map/train/pallas_call | solution.py:460
  39.3 1.2 %unpack.1 = (f32[64,864]{1,0:T(8,128)}, f32[64,1728]{1,0:T(8,128)}, bf16[16,16,1024]{2,1,0:T(8,128)(2,1)}) custom-call(bf16[512,128]{1,0:T(8,128)(2,1)S(1)} %get-tuple-element.9.total1_ref, bf16[1024,128]{1,0:T(8,128)(2,1)S(1)} %get-tuple-element.10.total2_ref, bf16[16,16,1024]{2,1,0:T(8,128)(2,1)S(1)} %get-tuple-element.11.dec_ref), custom_call_target="tpu_custom_call" | custom-call | tf_op jit(solution)/shard_map/unpack/pallas_call | solution.py:506

commit v7 on v6

--- a/solution.py
+++ b/solution.py
@@ -362,6 +362,13 @@
         self.home.wait_send()
 
 
+def turn(total_ref, count, ref):
+    row, col = iota((64, 128), 0), iota((64, 128), 1)
+    for half in range(2):
+        pick = jnp.where(col == row + 64 * half, 1.0, 0.0).astype(BF16)
+        ref[:, count * half : count * half + count] = dot(pick, total_ref[0:count], ((1,), (1,)))
+
+
 def total_scratch(rows):
     return [
         pltpu.VMEM((32 * rows, 128), F32),
@@ -376,10 +383,10 @@
 
 
 def train_kernel(factor, assign_hbm, occ_hbm, feats_hbm, w1_hbm, w2_hbm, cot_hbm,
-                 out1_ref, out2_ref, dec_ref,
+                 out1_ref, second_ref, dec_ref,
                  assign_ref, owner_ref, occ_ref, feats, w1, w2, cot, packed, stage, bricks,
                  fe, he, de, wide1, wide2, wide3, p1, p2, p3,
-                 load_sem, send_sem, recv_sem, *totals):
+                 out2, load_sem, send_sem, recv_sem, *totals):
     tile, scene = lax.axis_index("tile"), lax.axis_index("scene")
     barrier = pltpu.get_barrier_semaphore()
     for step, place in zip(FAR_FIRST, PLANE):
@@ -393,7 +400,7 @@
         load.start()
     pay1, pay2 = totals[0], totals[8]
     sum1 = Total(FIRST_ROWS, factor, pay1, out1_ref, *totals[1:8])
-    sum2 = Total(SECOND_ROWS, factor, pay2, out2_ref, *totals[9:16])
+    sum2 = Total(SECOND_ROWS, factor, pay2, out2, *totals[9:16])
 
     for load in loads[:3]:
         load.wait()
@@ -438,6 +445,7 @@
     sum2.back()
     sum1.back()
     sum2.finish()
+    turn(out2, 864, second_ref)
     sum1.finish()
     wait_bytes(bricks.at[pl.ds(0, SCENES - 1)], send_sem)
 
@@ -461,7 +469,7 @@
         functools.partial(train_kernel, factor),
         out_shape=[
             pltpu.VMEM((32 * FIRST_ROWS, 128), BF16),
-            pltpu.VMEM((32 * SECOND_ROWS, 128), BF16),
+            pltpu.VMEM((64, 1728), F32),
             pltpu.VMEM(cot.shape, BF16),
         ],
         in_specs=[anyspace] * 6,
@@ -478,6 +486,7 @@
             pltpu.VMEM((SCENES, 32, 256), BF16),
             pltpu.VMEM((SCENES, 32, 256), BF16),
             *compute_scratch(),
+            pltpu.VMEM((32 * SECOND_ROWS, 128), BF16),
             sem(10), pltpu.SemaphoreType.DMA, pltpu.SemaphoreType.DMA,
             *total_scratch(FIRST_ROWS),
             *total_scratch(SECOND_ROWS),
@@ -487,45 +496,41 @@
     )(*(pltpu.with_memory_space_constraint(x, pltpu.HBM) for x in (assign, planes, feats, w1, w2, cot)))
 
 
-def unpack_kernel(total1_ref, total2_ref, dec_ref, first_hbm, second_hbm, dec_hbm, first_ref, second_ref, sem):
-    stores = [pltpu.make_async_copy(dec_ref, dec_hbm, sem.at[0])]
+def unpack_kernel(total1_ref, second_ref, dec_ref, first_hbm, second_hbm, dec_hbm, first_ref, sem):
+    stores = [
+        pltpu.make_async_copy(dec_ref, dec_hbm, sem.at[0]),
+        pltpu.make_async_copy(second_ref, second_hbm, sem.at[1]),
+        pltpu.make_async_copy(first_ref, first_hbm, sem.at[2]),
+    ]
     stores[0].start()
-    row, col = iota((64, 128), 0), iota((64, 128), 1)
-    picks = [jnp.where(col == row + 64 * half, 1.0, 0.0).astype(BF16) for half in range(2)]
-    jobs = ((second_ref, second_hbm, total2_ref, 864), (first_ref, first_hbm, total1_ref, 432))
-    for at, (ref, hbm, total_ref, count) in enumerate(jobs):
-        for half in range(2):
-            ref[:, count * half : count * half + count] = dot(picks[half], total_ref[0:count], ((1,), (1,)))
-        stores.append(pltpu.make_async_copy(ref, hbm, sem.at[1 + at]))
-        stores[-1].start()
+    stores[1].start()
+    turn(total1_ref, 432, first_ref)
+    stores[2].start()
     for store in stores:
         store.wait()
 
 
-def unpack(total1, total2, decoded):
+def unpack(total1, second, decoded):
+    anyspace = pl.BlockSpec(memory_space=pl.ANY)
     return pl.pallas_call(
         unpack_kernel,
         out_shape=[
             jax.ShapeDtypeStruct((64, 864), F32),
-            jax.ShapeDtypeStruct((64, 1728), F32),
+            jax.ShapeDtypeStruct(second.shape, F32),
             jax.ShapeDtypeStruct(decoded.shape, BF16),
         ],
-        in_specs=[vmem(), vmem(), pl.BlockSpec(memory_space=pl.ANY)],
-        out_specs=[pl.BlockSpec(memory_space=pl.ANY)] * 3,
-        scratch_shapes=[
-            pltpu.VMEM((64, 864), F32),
-            pltpu.VMEM((64, 1728), F32),
-            pltpu.SemaphoreType.DMA((3,)),
-        ],
+        in_specs=[vmem(), anyspace, anyspace],
+        out_specs=[anyspace] * 3,
+        scratch_shapes=[pltpu.VMEM((64, 864), F32), pltpu.SemaphoreType.DMA((3,))],
         compiler_params=pltpu.CompilerParams(vmem_limit_bytes=VMEM_LIMIT),
         name="unpack",
-    )(total1, total2, decoded)
+    )(total1, second, decoded)
 
 
 def per_device(feats, occupancy, assign, w_first, w_second, grad_out):
     factor = 1.0 / math.sqrt(256 * 16 * 16 * 16)
-    total1, total2, compact = train(assign, occupancy, feats, w_first.T, w_second.T, grad_out[0], factor)
-    grad_first, grad_second, decoded = unpack(total1, total2, compact)
+    total1, second, planes = train(assign, occupancy, feats, w_first.T, w_second.T, grad_out[0], factor)
+    grad_first, grad_second, decoded = unpack(total1, second, planes)
     return decoded[None], grad_first.T, grad_second.T
 
 

time: 40.7 us -> 40.5 us (level)
  no operation moved by 1% of the time
where the time goes in v7:
time: 40.5 us; the launch traced here: 40.4 us
  Pallas kernels  39.7 us (98%)
  between operations  0.64 us (2%)
    pallas_call x1, Pallas kernels, train(): pl.pallas_call(functools.partial(train_kernel, factor), out_shape=[pltpu....  38.7 us
    pallas_call x1, Pallas kernels, unpack(): pl.pallas_call(unpack_kernel, out_shape=[jax.ShapeDtypeStruct((64, 864),...  1.04 us

profile of v7, /device:TPU:1, one launch (start us, length us, event | category | flops | bytes accessed | tf_op | source)
XLA Modules:
  0.0 40.4 jit_solution(14155796498904780634)
XLA Ops:
  0.6 38.7 %train.1 = (bf16[512,128]{1,0:T(8,128)(2,1)S(1)}, f32[64,1728]{1,0:T(8,128)S(1)}, bf16[16,16,1024]{2,1,0:T(8,128)(2,1)S(1)}) custom-call(s32[1,16]{1,0:T(1,128)} %assign_hbm.1, s32[4,4,4,16]{3,2,1,0:T(4,128)} %bitcast.10, bf16[16,2,32,1024]{3,2,1,0:T(8,128)(2,1)} %feats_hbm.1, bf16[64,864]{1,0:T(8,128)(2,1)} %bitcast.9, bf16[64,1728]{1,0:T(8,128)(2,1)} %bitcast.8, ...), custom_call_target="tpu_custom_call" | custom-call | tf_op jit(solution)/shard_map/train/pallas_call | solution.py:468
  39.3 1.0 %unpack.1 = (f32[64,864]{1,0:T(8,128)}, f32[64,1728]{1,0:T(8,128)}, bf16[16,16,1024]{2,1,0:T(8,128)(2,1)}) custom-call(bf16[512,128]{1,0:T(8,128)(2,1)S(1)} %get-tuple-element.9.total1_ref, f32[64,1728]{1,0:T(8,128)S(1)} %get-tuple-element.10.second_ref, bf16[16,16,1024]{2,1,0:T(8,128)(2,1)S(1)} %get-tuple-element.11.dec_ref), custom_call_target="tpu_custom_call" | custom-call | tf_op jit(solution)/shard_map/unpack/pallas_call | solution.py:515
